TPU v7x, 32 devices: a whole 2x2x4 slice. The times are simulated.
32 devices in a mesh: section: 2 (over x), dp: 16 (over z, y, core).
Axes of the slice: x: 2, y: 2, z: 4, core: 2. Of those that a mesh axis runs over, the one named last changes fastest.
Arguments:
- tokens: bfloat16 [32, 128, 768], P('dp'), may hold values from -6 to 6
- cotangent: bfloat16 [32, 128, 768], P('dp'), may hold values from -6 to 6
- page_lengths: int32 [32], P('dp'), may hold values from 1 to 128, 3072 in all
- cut_order: int32 [32, 128], P('dp'), may hold values from 0 to 127, each once within a row
- cut_region: int32 [32, 128], P('dp'), may hold values from 0 to 15, never falling along the last dimension, each value on 1 to 12 neighbouring positions
- cell_column: int32 [32, 128], P('dp'), may hold values from 0 to 63
- cell_row: int32 [32, 128], P('dp'), may hold values from 0 to 63
- input_proj: bfloat16 [2, 768, 2304], P('section'), may hold values from -0.21875 to 0.21875
- output_proj: bfloat16 [2, 768, 768], P('section'), may hold values from -0.875 to 0.875
- up_proj: bfloat16 [2, 768, 3072], P('section'), may hold values from -0.21875 to 0.21875
- down_proj: bfloat16 [2, 3072, 768], P('section'), may hold values from -0.109375 to 0.109375
- up_bias: bfloat16 [2, 3072], P('section'), may hold values from -4 to 4
- bias_rows: bfloat16 [2, 7, 768], P('section'), may hold values from -4 to 4
- gain_rows: bfloat16 [2, 2, 768], P('section'), may hold values from 0.25 to 1.75
- conv_taps: bfloat16 [2, 7, 768], P('section'), may hold values from -4 to 4
- bias_table: bfloat16 [2, 1920], P('section'), may hold values from -6 to 6
Outputs:
- layer_outputs: bfloat16 [2, 32, 128, 768], P('section', 'dp')
- input_grads: float32 [2, 32, 128, 768], P('section', 'dp')
- input_proj_grad: float32 [2, 768, 2304], P('section', 'dp')
- output_proj_grad: float32 [2, 768, 768], P('section', 'dp')
- up_proj_grad: float32 [2, 768, 3072], P('section', 'dp')
- down_proj_grad: float32 [2, 3072, 768], P('section', 'dp')
- up_bias_grad: float32 [2, 3072], P('section', 'dp')
- bias_rows_grad: float32 [2, 7, 768], P('section', None, 'dp')
- gain_rows_grad: float32 [2, 2, 768], P('section', None, 'dp')
- conv_taps_grad: float32 [2, 7, 768], P('section', None, 'dp')
- bias_table_grad: float32 [2, 1920], P('section', 'dp')
Inputs may be any that keep to these rules, and one draw needn't show every extreme that they name: `cut_order`: each row holds every slot 0 to 127 exactly once. `cut_region`: never falls along a row; a region spans at most 12 places. `page_lengths`: slots 0 to length - 1 of a page are live.
All inputs are finite; a program needn't handle non-finite values. No bound on the sum of `page_lengths` on one device may be relied on, other than what follows from the above.
Results may differ from a plain program's by a relative error of at most 0.025.
Values may be sent and summed in bfloat16 or wider, within the bound.
No kernel may reach another device: no remote copies, remote signals or barrier semaphores. Data moves between devices by JAX's collectives and lax.ppermute only.
A program may use at most 256 MiB of HBM per device.

v0:
```python
import jax
import jax.numpy as jnp
from jax import lax
from jax.sharding import PartitionSpec as P

HEADS = 12
HEAD = 64
B1D = 32
B2D = 64


norm_epsilon = 1e-05
masked_score = -1000000000.0
tap_reach = 3


def shifted_2(value, axis, by):
    count = lax.axis_size(axis)
    pairs = [(i, i + by) for i in range(count) if 0 <= i + by < count]
    return lax.ppermute(value, axis, pairs)


def shifted(values_in, offset):
    length_all = values_in.shape[0]
    padding = [(tap_reach, tap_reach)] + [(0, 0)] * (values_in.ndim - 1)
    padded = jnp.pad(values_in, padding)
    return padded[tap_reach + offset : tap_reach + offset + length_all]


def page_geometry(cut_order, cut_region, cell_column, cell_row, page_length):
    tokens_here = cut_order.shape[0]
    places = jnp.arange(tokens_here, dtype=jnp.int32)
    ranking = jnp.zeros((tokens_here,), jnp.int32).at[cut_order].set(places)
    live_order = cut_order < page_length
    ones_int = jnp.ones((tokens_here,), jnp.int32)
    tap_masks = []
    for offset in range(-tap_reach, tap_reach + 1):
        joined = (
            (shifted(ones_int, offset) > 0)
            & (shifted(cut_region, offset) == cut_region)
            & shifted(live_order, offset)
        )
        tap_masks.append(joined.astype(jnp.float32))
    key_live = places < page_length
    return (cut_order, ranking, jnp.stack(tap_masks), key_live, cell_column, cell_row)


def conv_apply(hidden, taps, geometry):
    cut_order, ranking, tap_masks = (geometry[0], geometry[1], geometry[2])
    ordered = jnp.take(hidden, cut_order, axis=0)
    mixed_sum = jnp.zeros_like(ordered)
    for column in range(2 * tap_reach + 1):
        mixed_sum = (
            mixed_sum
            + taps[column] * shifted(ordered, column - tap_reach) * tap_masks[column][:, None]
        )
    return jnp.take(mixed_sum, ranking, axis=0)


def conv_backward(grad_mixed, hidden, taps, geometry):
    cut_order, ranking, tap_masks = (geometry[0], geometry[1], geometry[2])
    grad_order = jnp.take(grad_mixed, cut_order, axis=0)
    ordered = jnp.take(hidden, cut_order, axis=0)
    tap_grads = []
    grad_source = jnp.zeros_like(ordered)
    for column in range(2 * tap_reach + 1):
        masked_grad = grad_order * tap_masks[column][:, None]
        tap_grads.append(jnp.sum(masked_grad * shifted(ordered, column - tap_reach), axis=0))
        grad_source = grad_source + shifted(taps[column] * masked_grad, tap_reach - column)
    return (jnp.take(grad_source, ranking, axis=0), jnp.stack(tap_grads))


def bucket_select(bucket_count):
    places = jnp.arange(bucket_count, dtype=jnp.int32)
    apart_bucket = jnp.clip(
        places[None, :] - places[:, None] + bucket_count // 2, 0, bucket_count - 1
    )
    return apart_bucket[:, :, None] == places[None, None, :]


def bias_pieces(geometry):
    ranking, cell_column, cell_row = (geometry[1], geometry[4], geometry[5])
    near_bucket = jnp.clip(ranking[None, :] - ranking[:, None] + B1D // 2, 0, B1D - 1)
    near_hot = (near_bucket[:, :, None] == jnp.arange(B1D, dtype=jnp.int32)[None, None, :]).astype(
        jnp.bfloat16
    )
    cell_range = jnp.arange(B2D, dtype=jnp.int32)[None, :]
    column_hot = (cell_column[:, None] == cell_range).astype(jnp.bfloat16)
    row_hot = (cell_row[:, None] == cell_range).astype(jnp.bfloat16)
    return (near_hot, column_hot, row_hot)


def relative_bias(bias_table, geometry):
    lookup = bias_table.reshape(B1D + 2 * B2D, HEADS)
    near_hot, column_hot, row_hot = bias_pieces(geometry)
    selector = bucket_select(B2D).astype(jnp.bfloat16)
    result = jnp.einsum("qkb,bh->hqk", near_hot, lookup[:B1D], preferred_element_type=jnp.float32)
    for cell_hot, first_row in ((column_hot, B1D), (row_hot, B1D + B2D)):
        grid = jnp.einsum(
            "uvb,bh->huv",
            selector,
            lookup[first_row : first_row + B2D],
            preferred_element_type=jnp.float32,
        ).astype(jnp.bfloat16)
        rows_part = jnp.einsum(
            "qu,huv->hqv", cell_hot, grid, preferred_element_type=jnp.float32
        ).astype(jnp.bfloat16)
        result = result + jnp.einsum(
            "hqv,kv->hqk", rows_part, cell_hot, preferred_element_type=jnp.float32
        )
    return result


def table_grad(grad_scores, geometry):
    near_hot, column_hot, row_hot = bias_pieces(geometry)
    selector = bucket_select(B2D).astype(jnp.float32)
    pieces = [jnp.einsum("hqk,qkb->bh", grad_scores, near_hot, preferred_element_type=jnp.float32)]
    for cell_hot in (column_hot, row_hot):
        along = jnp.einsum("hqk,kv->hqv", grad_scores, cell_hot, preferred_element_type=jnp.float32)
        grid_grad = jnp.einsum(
            "qu,hqv->huv", cell_hot.astype(jnp.float32), along, precision=lax.Precision.HIGHEST
        )
        pieces.append(
            jnp.einsum("uvb,huv->bh", selector, grid_grad, precision=lax.Precision.HIGHEST)
        )
    return jnp.concatenate(pieces, axis=0).reshape(-1)


def normalize(hidden):
    average = jnp.mean(hidden, axis=-1, keepdims=True)
    centered = hidden - average
    spread = jnp.mean(centered * centered, axis=-1, keepdims=True)
    inv_scale = lax.rsqrt(spread + norm_epsilon)
    return (centered * inv_scale, inv_scale)


def norm_back(grad_norm, normed, inv_scale):
    first_mean = jnp.mean(grad_norm, axis=-1, keepdims=True)
    second_mean = jnp.mean(grad_norm * normed, axis=-1, keepdims=True)
    return inv_scale * (grad_norm - first_mean - normed * second_mean)


def gelu_slope(gate_in):
    normal_cdf = 0.5 * (1.0 + jax.scipy.special.erf(gate_in * 0.7071067811865476))
    return normal_cdf + gate_in * jnp.exp(-0.5 * gate_in * gate_in) * 0.3989422804014327


def split_heads(packed):
    model_width = packed.shape[1] // 3
    queries = packed[:, :model_width].reshape(-1, HEADS, HEAD)
    keys_all = packed[:, model_width : 2 * model_width].reshape(-1, HEADS, HEAD)
    values_all = packed[:, 2 * model_width :].reshape(-1, HEADS, HEAD)
    return (queries, keys_all, values_all)


def attention_scores(packed, bias, key_live):
    queries, keys_all, values_all = split_heads(packed)
    scores = (
        jnp.einsum("qhd,khd->hqk", queries, keys_all, preferred_element_type=jnp.float32)
        * HEAD ** (-0.5)
        + bias
    )
    return jnp.where(key_live[None, None, :], scores, masked_score)


def layer_forward(layer_in, weights, geometry, conv_on):
    (
        input_proj,
        output_proj,
        up_proj,
        down_proj,
        up_bias,
        bias_rows,
        gain_rows,
        conv_taps,
        bias_table,
    ) = weights
    bias_float = bias_rows.astype(jnp.float32)
    gain_float = gain_rows.astype(jnp.float32)
    hidden = layer_in.astype(jnp.float32)
    model_width = hidden.shape[1]
    mixed = hidden + conv_on * (
        conv_apply(hidden, conv_taps.astype(jnp.float32), geometry) + bias_float[6]
    )
    mixed_low = mixed.astype(jnp.bfloat16)
    projected = jnp.dot(mixed_low, input_proj, preferred_element_type=jnp.float32)
    packed = jnp.concatenate(
        [
            projected[:, :model_width] + bias_float[0],
            projected[:, model_width : 2 * model_width],
            projected[:, 2 * model_width :] + bias_float[1],
        ],
        axis=1,
    ).astype(jnp.bfloat16)
    bias = relative_bias(bias_table, geometry)
    scores = attention_scores(packed, bias, geometry[3])
    highest = jnp.max(scores, axis=-1, keepdims=True)
    expo = jnp.exp(scores - highest)
    totals = jnp.sum(expo, axis=-1, keepdims=True)
    probs = expo / totals
    log_totals = highest + jnp.log(totals)
    values_all = split_heads(packed)[2]
    attended = (
        jnp.einsum(
            "hqk,khd->qhd",
            probs.astype(jnp.bfloat16),
            values_all,
            preferred_element_type=jnp.float32,
        )
        .reshape(-1, model_width)
        .astype(jnp.bfloat16)
    )
    branch = jnp.dot(attended, output_proj, preferred_element_type=jnp.float32) + bias_float[2]
    first_norm, first_scale = normalize(mixed + branch)
    first = first_norm * gain_float[0] + bias_float[3]
    first_low = first.astype(jnp.bfloat16)
    gate_in = jnp.dot(first_low, up_proj, preferred_element_type=jnp.float32) + up_bias.astype(
        jnp.float32
    )
    activated = jax.nn.gelu(gate_in, approximate=False).astype(jnp.bfloat16)
    second = jnp.dot(activated, down_proj, preferred_element_type=jnp.float32) + bias_float[4]
    second_norm, second_scale = normalize(first + second)
    result = second_norm * gain_float[1] + bias_float[5]
    kept_items = (
        layer_in,
        mixed_low,
        packed,
        bias,
        log_totals,
        attended,
        first_norm,
        first_scale,
        first_low,
        gate_in,
        activated,
        second_norm,
        second_scale,
    )
    return (result.astype(jnp.bfloat16), kept_items)


def blank_kept(micro_count, tokens_here, model_width, hidden_width):
    plain = jnp.bfloat16
    wide = jnp.float32
    layouts = [
        ((tokens_here, model_width), plain),
        ((tokens_here, model_width), plain),
        ((tokens_here, 3 * model_width), plain),
        ((HEADS, tokens_here, tokens_here), wide),
        ((HEADS, tokens_here, 1), wide),
        ((tokens_here, model_width), plain),
        ((tokens_here, model_width), wide),
        ((tokens_here, 1), wide),
        ((tokens_here, model_width), plain),
        ((tokens_here, hidden_width), wide),
        ((tokens_here, hidden_width), plain),
        ((tokens_here, model_width), wide),
        ((tokens_here, 1), wide),
    ]
    return tuple(
        (jnp.zeros((micro_count,) + dims_here, kind_here) for dims_here, kind_here in layouts)
    )


def layer_backward(grad_out, kept_items, weights, geometry, conv_on):
    (
        input_proj,
        output_proj,
        up_proj,
        down_proj,
        up_bias,
        bias_rows,
        gain_rows,
        conv_taps,
        bias_table,
    ) = weights
    (
        layer_in,
        mixed_low,
        packed,
        bias,
        log_totals,
        attended,
        first_norm,
        first_scale,
        first_low,
        gate_in,
        activated,
        second_norm,
        second_scale,
    ) = kept_items
    gain_float = gain_rows.astype(jnp.float32)
    model_width = layer_in.shape[1]
    grad_sum = norm_back(grad_out * gain_float[1], second_norm, second_scale)
    grad_second = grad_sum.astype(jnp.bfloat16)
    grad_act = jnp.einsum("sd,fd->sf", grad_second, down_proj, preferred_element_type=jnp.float32)
    grad_gate = (grad_act * gelu_slope(gate_in)).astype(jnp.bfloat16)
    grad_first = grad_sum + jnp.einsum(
        "sf,df->sd", grad_gate, up_proj, preferred_element_type=jnp.float32
    )
    grad_mid = norm_back(grad_first * gain_float[0], first_norm, first_scale)
    grad_branch = grad_mid.astype(jnp.bfloat16)
    grad_attended = jnp.einsum(
        "sd,ed->se", grad_branch, output_proj, preferred_element_type=jnp.float32
    ).astype(jnp.bfloat16)
    queries, keys_all, values_all = split_heads(packed)
    scores = attention_scores(packed, bias, geometry[3])
    probs = jnp.exp(scores - log_totals)
    grad_heads = grad_attended.reshape(-1, HEADS, HEAD)
    grad_probs = jnp.einsum(
        "qhd,khd->hqk", grad_heads, values_all, preferred_element_type=jnp.float32
    )
    inner = jnp.sum(probs * grad_probs, axis=-1, keepdims=True)
    grad_scores = (probs * (grad_probs - inner)).astype(jnp.bfloat16)
    scale_factor = HEAD ** (-0.5)
    grad_queries = (
        jnp.einsum("hqk,khd->qhd", grad_scores, keys_all, preferred_element_type=jnp.float32)
        * scale_factor
    )
    grad_keys = (
        jnp.einsum("hqk,qhd->khd", grad_scores, queries, preferred_element_type=jnp.float32)
        * scale_factor
    )
    grad_values = jnp.einsum(
        "hqk,qhd->khd", probs.astype(jnp.bfloat16), grad_heads, preferred_element_type=jnp.float32
    )
    grad_packed = jnp.concatenate(
        [
            grad_queries.reshape(-1, model_width),
            grad_keys.reshape(-1, model_width),
            grad_values.reshape(-1, model_width),
        ],
        axis=1,
    ).astype(jnp.bfloat16)
    grad_mixed = grad_mid + jnp.einsum(
        "se,de->sd", grad_packed, input_proj, preferred_element_type=jnp.float32
    )
    hidden = layer_in.astype(jnp.float32)
    grad_conv_in, grad_taps = conv_backward(
        grad_mixed, hidden, conv_taps.astype(jnp.float32), geometry
    )
    grad_in = grad_mixed + conv_on * grad_conv_in
    packed_float = grad_packed.astype(jnp.float32)
    bias_grads = jnp.stack(
        [
            jnp.sum(packed_float[:, :model_width], axis=0),
            jnp.sum(packed_float[:, 2 * model_width :], axis=0),
            jnp.sum(grad_branch.astype(jnp.float32), axis=0),
            jnp.sum(grad_first, axis=0),
            jnp.sum(grad_second.astype(jnp.float32), axis=0),
            jnp.sum(grad_out, axis=0),
            conv_on * jnp.sum(grad_mixed, axis=0),
        ]
    )
    gain_grads = jnp.stack(
        [jnp.sum(grad_first * first_norm, axis=0), jnp.sum(grad_out * second_norm, axis=0)]
    )
    up_grad = jnp.sum(grad_gate.astype(jnp.float32), axis=0)
    small_terms = (
        up_grad,
        bias_grads,
        gain_grads,
        conv_on * grad_taps,
        table_grad(grad_scores, geometry),
    )
    return (grad_in, (grad_packed, grad_branch, grad_gate, grad_second), small_terms)


def weight_terms(kept_items, grad_parts, small_terms):
    mixed_low, attended, first_low, activated = (
        kept_items[1],
        kept_items[5],
        kept_items[8],
        kept_items[10],
    )
    grad_packed, grad_branch, grad_gate, grad_second = grad_parts
    input_term = jnp.einsum("sd,se->de", mixed_low, grad_packed, preferred_element_type=jnp.float32)
    output_term = jnp.einsum("sd,se->de", attended, grad_branch, preferred_element_type=jnp.float32)
    up_term = jnp.einsum("sd,sf->df", first_low, grad_gate, preferred_element_type=jnp.float32)
    down_term = jnp.einsum("sf,sd->fd", activated, grad_second, preferred_element_type=jnp.float32)
    return (input_term, output_term, up_term, down_term) + tuple(small_terms)


def pick(stacked_tree, position):
    return jax.tree.map(
        lambda stacked: lax.dynamic_index_in_dim(stacked, position, 0, keepdims=False), stacked_tree
    )


def place(stacked_tree, new_tree, position):
    return jax.tree.map(
        lambda stacked, element: lax.dynamic_update_index_in_dim(stacked, element, position, 0),
        stacked_tree,
        new_tree,
    )


def local(
    tokens,
    cotangent,
    page_lengths,
    cut_order,
    cut_region,
    cell_column,
    cell_row,
    input_proj,
    output_proj,
    up_proj,
    down_proj,
    up_bias,
    bias_rows,
    gain_rows,
    conv_taps,
    bias_table,
):
    weights = tuple(
        (
            stacked[0]
            for stacked in (
                input_proj,
                output_proj,
                up_proj,
                down_proj,
                up_bias,
                bias_rows,
                gain_rows,
                conv_taps,
                bias_table,
            )
        )
    )
    section_index = lax.axis_index("section")
    section_count = lax.axis_size("section")
    conv_on = (section_index == 0).astype(jnp.float32)
    micro_count = tokens.shape[0]
    tokens_here = tokens.shape[1]
    model_width = tokens.shape[2]
    hidden_width = up_proj.shape[2]
    geometries = jax.vmap(page_geometry)(cut_order, cut_region, cell_column, cell_row, page_lengths)
    tick_count = micro_count + section_count - 1
    kept_all = blank_kept(micro_count, tokens_here, model_width, hidden_width)
    layer_out = jnp.zeros((micro_count, tokens_here, model_width), jnp.bfloat16)
    arrived = jnp.zeros((tokens_here, model_width), jnp.bfloat16)
    for moment in range(tick_count):
        micro_index = moment - section_index
        active = (micro_index >= 0) & (micro_index < micro_count)
        position = jnp.clip(micro_index, 0, micro_count - 1)
        own_tokens = lax.dynamic_index_in_dim(tokens, position, 0, keepdims=False)
        layer_in = jnp.where(section_index == 0, own_tokens, arrived)

        def forward_step(carried):
            kept_now, out_now = carried
            result, kept_items = layer_forward(
                layer_in, weights, pick(geometries, position), conv_on
            )
            return (
                place(kept_now, kept_items, position),
                lax.dynamic_update_index_in_dim(out_now, result, position, 0),
            )

        kept_all, layer_out = lax.cond(
            active, forward_step, lambda carried: carried, (kept_all, layer_out)
        )
        if moment < tick_count - 1:
            leaving = lax.dynamic_index_in_dim(layer_out, position, 0, keepdims=False)
            arrived = shifted_2(leaving, "section", 1)
    zero_terms = tuple((jnp.zeros(item_w.shape, jnp.float32) for item_w in weights))
    grad_buffer = jnp.zeros((micro_count, tokens_here, model_width), jnp.float32)
    arrived_grad = jnp.zeros((tokens_here, model_width), jnp.bfloat16)
    totals = None
    for moment in range(tick_count):
        micro_index = moment - (section_count - 1 - section_index)
        active = (micro_index >= 0) & (micro_index < micro_count)
        position = jnp.clip(micro_index, 0, micro_count - 1)
        top_grad = lax.dynamic_index_in_dim(cotangent, position, 0, keepdims=False)
        grad_out = jnp.where(section_index == section_count - 1, top_grad, arrived_grad).astype(
            jnp.float32
        )
        running = zero_terms if totals is None else totals

        def backward_into(carried):
            buffer_now, totals_now = carried
            kept_items = pick(kept_all, position)
            grad_in, grad_parts, small_terms = layer_backward(
                grad_out, kept_items, weights, pick(geometries, position), conv_on
            )
            terms = weight_terms(kept_items, grad_parts, small_terms)
            return (
                lax.dynamic_update_index_in_dim(buffer_now, grad_in, position, 0),
                tuple((earlier + later for earlier, later in zip(totals_now, terms))),
            )

        grad_buffer, totals = lax.cond(
            active, backward_into, lambda carried: carried, (grad_buffer, running)
        )
        if moment < tick_count - 1:
            leaving_grad = lax.dynamic_index_in_dim(
                grad_buffer, position, 0, keepdims=False
            ).astype(jnp.bfloat16)
            arrived_grad = shifted_2(leaving_grad, "section", -1)
    shares = (
        lax.psum_scatter(totals[0], "dp", scatter_dimension=0, tiled=True),
        lax.psum_scatter(totals[1], "dp", scatter_dimension=0, tiled=True),
        lax.psum_scatter(totals[2], "dp", scatter_dimension=0, tiled=True),
        lax.psum_scatter(totals[3], "dp", scatter_dimension=0, tiled=True),
        lax.psum_scatter(totals[4], "dp", scatter_dimension=0, tiled=True),
        lax.psum_scatter(totals[5], "dp", scatter_dimension=1, tiled=True),
        lax.psum_scatter(totals[6], "dp", scatter_dimension=1, tiled=True),
        lax.psum_scatter(totals[7], "dp", scatter_dimension=1, tiled=True),
        lax.psum_scatter(totals[8], "dp", scatter_dimension=0, tiled=True),
    )
    return (
        layer_out[None],
        grad_buffer[None],
        shares[0][None],
        shares[1][None],
        shares[2][None],
        shares[3][None],
        shares[4][None],
        shares[5][None],
        shares[6][None],
        shares[7][None],
        shares[8][None],
    )


def solution(mesh):
    placed = (
        P("dp", None, None),
        P("dp", None, None),
        P("dp"),
        P("dp", None),
        P("dp", None),
        P("dp", None),
        P("dp", None),
        P("section", None, None),
        P("section", None, None),
        P("section", None, None),
        P("section", None, None),
        P("section", None),
        P("section", None, None),
        P("section", None, None),
        P("section", None, None),
        P("section", None),
    )
    return jax.shard_map(
        local,
        mesh=mesh,
        in_specs=placed,
        out_specs=(
            P("section", "dp", None, None),
            P("section", "dp", None, None),
            P("section", "dp", None),
            P("section", "dp", None),
            P("section", "dp", None),
            P("section", "dp", None),
            P("section", "dp"),
            P("section", None, "dp"),
            P("section", None, "dp"),
            P("section", None, "dp"),
            P("section", "dp"),
        ),
        check_vma=False,
    )
```

profile of v0, /device:TPU:0, one launch (start us, length us, event | category | flops | bytes accessed | tf_op | source)
XLA Modules:
  0.0 1169.2 jit_solution(10664504326974110156)
XLA Ops:
  16.8 11.4 scatter_fusion
  28.3 62.1 %conditional.6 = (bf16[2,128,768]{2,1,0:T(8,128)(2,1)}, bf16[2,128,768]{2,1,0:T(8,128)(2,1)}, bf16[2,128,2304]{2,1,0:T(8,128)(2,1)}, f32[2,12,128,128]{3,1,2,0:T...) conditional(s32[]{:T(128)} %convert_element_type.531, () %tuple.56, ...), branch_computations={%region_1.2_spmd, %region_2.10_spmd} | conditional | flops 2002040960 | bytes 114062552 | solution.py:461
  31.5 2.7 fusion.47
  57.6 4.8 bitcast_dynamic-update-slice_fusion
  63.7 4.1 bitcast_dynamic-update-slice_fusion.2
  93.4 4.4 collective-permute-done
  97.8 74.7 %conditional.7 = ((bf16[2,128,768]{2,1,0:T(8,128)(2,1)}, bf16[2,128,768]{2,1,0:T(8,128)(2,1)}, bf16[2,128,2304]{2,1,0:T(8,128)(2,1)}, f32[2,12,128,128]{3,1,2,0:...) conditional(s32[]{:T(128)} %convert_element_type.530, ...), branch_computations={%region_9.11_spmd, %region_10.18_spmd.clone.clone} | conditional | flops 2002139264 | bytes 81470536 | solution.py:461
  100.2 2.7 gather_fusion.11
  105.4 2.7 gather_fusion.12
  108.8 2.8 fusion.348
  121.0 2.5 copy.286
  128.0 2.6 copy.281
  134.8 2.5 copy.283
  150.8 4.4 bitcast_dynamic-update-slice_fusion.12
  155.2 4.1 bitcast_dynamic-update-slice_fusion.14
  173.4 20.3 %collective-permute-start.1 = (bf16[128,768]{1,0:T(8,128)(2,1)S(1)}, bf16[128,768]{1,0:T(8,128)(2,1)}, u32[]{:S(2)}, u32[]{:S(2)}) collective-permute-start(bf16[128,768]{1,0:T(8,128)(2,1)S(1)} %dynamic-slice_bitcast_fusion.6), channel_id=1, source_target_pairs={{0,16},{1,17},{2,18},{3,19},{4,20},{5,21},{6,22},{7,23},{8,24},{9,... | collective-permute-start | bytes 589832 | tf_op jit(solution)/shard_map/ppermute | solution.py:20
  198.9 20.3 %conditional.9 = (f32[2,128,768]{2,1,0:T(8,128)}, f32[768,2304]{1,0:T(8,128)}, f32[768,768]{1,0:T(8,128)S(1)}, f32[768,3072]{1,0:T(8,128)}, f32[3072,768]{1,0:T(...) conditional(s32[]{:T(128)} %convert_element_type.535, () %tuple.61, ...), branch_computations={%region_25.27_spmd, %region_26.0_spmd} | conditional | flops 4061201664 | bytes 153509968 | solution.py:493
  198.9 4.8 broadcast_in_dim.374
  203.7 4.3 broadcast_in_dim.375
  208.0 3.3 broadcast_in_dim.372
  222.3 133.1 %collective-permute-done.2 = bf16[128,768]{1,0:T(8,128)(2,1)} collective-permute-done((bf16[128,768]{1,0:T(8,128)(2,1)}, bf16[128,768]{1,0:T(8,128)(2,1)}, u32[]{:S(2)}, u32[]{:S(2)}) %collective-permute-start.2) | collective-permute-done | bytes 196640 | tf_op jit(solution)/shard_map/ppermute | solution.py:20
  357.2 130.7 %conditional.10 = ((f32[2,128,768]{2,1,0:T(8,128)}, f32[768,2304]{1,0:T(8,128)}, f32[768,768]{1,0:T(8,128)S(1)}, f32[768,3072]{1,0:T(8,128)}, f32[3072,768]{1,0:...) conditional(s32[]{:T(128)} %convert_element_type.534, ...), branch_computations={%region_49.51_spmd, %region_50.74_spmd} | conditional | flops 4068296704 | bytes 185208288 | solution.py:493
  362.4 5.3 convert_reduce_fusion.3
  367.8 3.7 fusion.184
  386.5 3.2 copy.228
  394.5 2.6 fusion.478
  398.3 2.8 gather_fusion.5
  402.8 2.8 gather_fusion.7
  431.8 2.7 fusion.167
  449.1 7.5 convolution_add_fusion.5
  458.6 2.8 gather_fusion.6
  463.5 9.0 convolution_add_fusion.7
  472.5 9.0 convolution_add_fusion.6
  490.8 6.6 collective-permute-done.3
  499.2 96.7 %conditional.11 = (f32[768,2304]{1,0:T(8,128)}, f32[768,768]{1,0:T(8,128)S(1)}, f32[768,3072]{1,0:T(8,128)}, f32[3072,768]{1,0:T(8,128)}, f32[3072]{0:T(1024)}, ...) conditional(s32[]{:T(128)} %convert_element_type.533, ...), branch_computations={%region_73.75_spmd, %region_74.98_spmd} | conditional | flops 4068297216 | bytes 174887632 | solution.py:493
  504.5 5.3 convert_reduce_fusion.6
  509.8 3.7 fusion.260
  525.9 2.7 copy.233
  566.3 7.2 convolution_add_fusion.11
  573.5 8.9 convolution_add_fusion.13
  586.9 9.0 convolution_add_fusion.12
  605.5 57.8 %all-reduce.29 = (f32[3072]{0:T(1024)S(1)}, f32[1920]{0:T(1024)S(1)}) all-reduce(f32[3072]{0:T(1024)} %get-tuple-element.855, f32[1920]{0:T(1024)} %get-tuple-element.859), channel_id=6, replica_groups=mesh['section'=2,'dp'=16] {'dp'}, use_global_device_ids=true, to_apply=%region_101.103.clone | all-reduce | flops 4992 | bytes 39936
  665.8 46.2 %reduce-scatter.22.cloned.1.call-done = f32[48,7]{1,0:T(8,128)} async-done(((f32[768,7]{1,0:T(8,128)}), f32[48,7]{1,0:T(8,128)}) %reduce-scatter.22.cloned.1.call-update) | async-done | bytes 1360
  713.4 56.8 %reduce-scatter.26.cloned.1.call-done = f32[48,7]{1,0:T(8,128)} async-done(((f32[768,7]{1,0:T(8,128)}), f32[48,7]{1,0:T(8,128)}) %reduce-scatter.26.cloned.1.call-update) | async-done | bytes 1360
  771.6 65.3 %reduce-scatter.16.cloned.1.call-done = f32[48,768]{1,0:T(8,128)} async-done(((f32[768,768]{1,0:T(8,128)}), f32[48,768]{1,0:T(8,128)}) %reduce-scatter.16.cloned.1.call-update) | async-done | bytes 147472 | tf_op jit(solution)/shard_map/reduce_scatter | solution.py:503
  836.9 93.5 %reduce-scatter.14.cloned.1.call-done = f32[48,2304]{1,0:T(8,128)} async-done(((f32[768,2304]{1,0:T(8,128)}), f32[48,2304]{1,0:T(8,128)}) %reduce-scatter.14.cloned.1.call-update) | async-done | bytes 442384 | tf_op jit(solution)/shard_map/reduce_scatter | solution.py:502
  930.4 116.0 %reduce-scatter.18.cloned.1.call-done = f32[48,3072]{1,0:T(8,128)} async-done(((f32[768,3072]{1,0:T(8,128)}), f32[48,3072]{1,0:T(8,128)}) %reduce-scatter.18.cloned.1.call-update) | async-done | bytes 589840 | tf_op jit(solution)/shard_map/reduce_scatter | solution.py:504
  1046.4 115.8 %reduce-scatter.20.cloned.1.call-done = f32[192,768]{1,0:T(8,128)} async-done(((f32[3072,768]{1,0:T(8,128)}), f32[192,768]{1,0:T(8,128)}) %reduce-scatter.20.cloned.1.call-update) | async-done | bytes 589840 | tf_op jit(solution)/shard_map/reduce_scatter | solution.py:505
  (651 shorter events, 283.3 us)
Async XLA Ops:
  7.2 21.1 %copy-start.123 = (s32[2,128]{1,0:T(2,128)S(1)}, s32[2,128]{1,0:T(2,128)}, u32[]{:S(2)}) copy-start(s32[2,128]{1,0:T(2,128)} %param.33) | copy-start | bytes 3076
  7.2 21.1 %copy-start.94 = (bf16[1,7,768]{2,1,0:T(8,128)(2,1)S(1)}, bf16[1,7,768]{2,1,0:T(8,128)(2,1)}, u32[]{:S(2)}) copy-start(bf16[1,7,768]{2,1,0:T(8,128)(2,1)} %param.44) | copy-start | bytes 32260
  7.2 21.1 %copy-start = (bf16[1,768,768]{2,1,0:T(8,128)(2,1)S(1)}, bf16[1,768,768]{2,1,0:T(8,128)(2,1)}, u32[]{:S(2)}) copy-start(bf16[1,768,768]{2,1,0:T(8,128)(2,1)} %param.38) | copy-start | bytes 3538948
  7.2 21.1 %copy-start.102 = (bf16[1,2,768]{2,1,0:T(2,128)(2,1)S(1)}, bf16[1,2,768]{2,1,0:T(2,128)(2,1)}, u32[]{:S(2)}) copy-start(bf16[1,2,768]{2,1,0:T(2,128)(2,1)} %param.43) | copy-start | bytes 9220
  7.2 21.1 %copy-start.99 = (bf16[1,7,768]{2,1,0:T(8,128)(2,1)S(1)}, bf16[1,7,768]{2,1,0:T(8,128)(2,1)}, u32[]{:S(2)}) copy-start(bf16[1,7,768]{2,1,0:T(8,128)(2,1)} %param.42) | copy-start | bytes 32260
  7.2 657.2 %reduce-scatter.24.cloned.1.call-start = ((), (), s32[]{:S(2)}) async-start(), calls=%async_computation.12 | async-start | bytes 417792
  14.5 13.8 %copy-start.95 = (f32[2,7,128]{2,0,1:T(2,128)}, f32[2,7,128]{2,0,1:T(2,128)S(1)}, u32[]{:S(2)}) copy-start(f32[2,7,128]{2,0,1:T(2,128)S(1)} %convert_bitcast_fusion) | copy-start | bytes 21508
  55.6 12.2 %slice-start.6 = ((s8[4718592]{0:T(1024)(128)(4,1)}), s8[4194304]{0:T(1024)(128)(4,1)S(1)}, s32[]{:S(2)}) async-start(s8[4718592]{0:T(1024)(128)(4,1)} %bitcast.952), calls=%async_computation.20 | async-start | bytes 8388608 | tf_op jit(solution)/shard_map/cond
  57.6 10.2 slice-start.7
  71.6 6.4 copy-start.60
  91.4 6.3 collective-permute-start
  148.8 6.4 copy-start.58
  148.8 10.5 slice-start.8
  150.8 8.6 slice-start.9
  173.4 23.8 %collective-permute-start.1 = (bf16[128,768]{1,0:T(8,128)(2,1)S(1)}, bf16[128,768]{1,0:T(8,128)(2,1)}, u32[]{:S(2)}, u32[]{:S(2)}) collective-permute-start(bf16[128,768]{1,0:T(8,128)(2,1)S(1)} %dynamic-slice_bitcast_fusion.6), channel_id=1, source_target_pairs={{0,16},{1,17},{2,18},{3,19},{4,20},{5,21},{6,22},{7,23},{8,24},{9,... | collective-permute-start | bytes 589832 | tf_op jit(solution)/shard_map/ppermute | solution.py:20
  221.0 134.4 %collective-permute-start.2 = (bf16[128,768]{1,0:T(8,128)(2,1)}, bf16[128,768]{1,0:T(8,128)(2,1)}, u32[]{:S(2)}, u32[]{:S(2)}) collective-permute-start(bf16[128,768]{1,0:T(8,128)(2,1)} %fusion.439), channel_id=1, source_target_pairs={{16,0},{17,1},{18,2},{19,3},{20,4},{21,5},{22,6},{23,7},{24,8},{25... | collective-permute-start | bytes 589832 | tf_op jit(solution)/shard_map/ppermute | solution.py:20
  360.4 7.3 slice-start.2
  449.0 7.6 copy-start.17
  449.0 7.6 copy-start.79
  449.0 7.6 copy-start.80
  449.0 7.6 copy-start.81
  449.0 7.6 copy-start.85
  449.1 7.6 copy-start.86
  449.1 7.6 copy-start.87
  449.1 7.6 copy-start.127
  449.1 7.6 copy-start.165
  449.1 7.6 copy-start.176
  463.5 9.0 copy-start.31
  489.5 7.9 collective-permute-start.3
  502.5 7.3 slice-start.4
  520.8 7.9 copy-start.63
  520.8 7.9 copy-start.67
  547.0 6.4 copy-start.147
  547.0 6.4 copy-start.144
  547.0 6.4 copy-start.143
  547.0 7.8 copy-start.183
  547.0 7.8 copy-start.188
  559.8 6.5 copy-start.46
  559.8 6.5 copy-start.49
  559.8 6.5 copy-start.51
  566.3 7.2 copy-start.42
  573.5 10.1 copy-start.38
  597.6 114.4 %reduce-scatter.22.cloned.1.call-start = ((), (), s32[]{:S(2)}) async-start(), calls=%async_computation.11 | async-start | bytes 417792
  599.3 170.8 %reduce-scatter.26.cloned.1.call-start = ((), (), s32[]{:S(2)}) async-start(), calls=%async_computation.13 | async-start | bytes 417792
  601.1 235.8 %reduce-scatter.16.cloned.1.call-start = ((), (), s32[]{:S(2)}) async-start(), calls=%async_computation.8 | async-start | bytes 2506752 | tf_op jit(solution)/shard_map/reduce_scatter | solution.py:503
  601.7 328.7 %reduce-scatter.14.cloned.1.call-start = ((), (), s32[]{:S(2)}) async-start(), calls=%async_computation.7 | async-start | bytes 7520256 | tf_op jit(solution)/shard_map/reduce_scatter | solution.py:502
  602.3 444.1 %reduce-scatter.18.cloned.1.call-start = ((), (), s32[]{:S(2)}) async-start(), calls=%async_computation.9 | async-start | bytes 10027008 | tf_op jit(solution)/shard_map/reduce_scatter | solution.py:504
  602.8 559.3 %reduce-scatter.20.cloned.1.call-start = ((), (), s32[]{:S(2)}) async-start(), calls=%async_computation.10 | async-start | bytes 10027008 | tf_op jit(solution)/shard_map/reduce_scatter | solution.py:505
  (104 other events, 293.5 us)
Sparse Core Ops, SparseCore 0:
  597.7 55.7 reduce-scatter.23
  657.3 54.6 reduce-scatter.21
  715.5 54.6 reduce-scatter.25
  774.8 61.9 reduce-scatter.15
  841.3 89.0 reduce-scatter.13
  935.4 110.8 reduce-scatter.17
  1051.0 111.0 reduce-scatter.19
where the time goes:
time: 1180 us; the launch traced here: 1170 us
  waiting for transfers between devices  642 us (54%)
  local copies, waits for them, and re-layouts  179 us (15%)
  matrix products  143 us (12%)
  other arithmetic  99.9 us (8%)
  blocking collectives  57.8 us (5%)
  starting transfers between devices  25.1 us (2%)
  between operations  15.9 us (1%)
    ppermute x4, waiting for transfers between devices, shifted_2(): return lax.ppermute(value, axis, pairs)  146 us
    reduce_scatter x1, waiting for transfers between devices, local(): lax.psum_scatter(totals[2], 'dp', scatter_dimension=0, tiled=True)  116 us
    reduce_scatter x1, waiting for transfers between devices, local(): lax.psum_scatter(totals[3], 'dp', scatter_dimension=0, tiled=True)  116 us
    unnamed x10, waiting for transfers between devices  105 us
    reduce_scatter x1, waiting for transfers between devices, local(): lax.psum_scatter(totals[0], 'dp', scatter_dimension=0, tiled=True)  93.5 us
    reduce_scatter x1, waiting for transfers between devices, local(): lax.psum_scatter(totals[1], 'dp', scatter_dimension=0, tiled=True)  65.3 us
    unnamed x1, blocking collectives  57.8 us
    another operation x32, local copies, waits for them, and re-layouts  35.7 us
  transfers between devices with their start and end apart: 11, of which 10 were waited for; matrix products, arithmetic and copies ran while one was open for 1% of the time, Pallas kernels for 0%

commit v1 on v0

v1 whole, which is shorter than its diff:
```python
import functools

import jax
import jax.numpy as jnp
from jax import lax
from jax.experimental import pallas as pl
from jax.experimental.pallas import tpu as pltpu
from jax.sharding import PartitionSpec as P

HEADS = 12
HEAD = 64
B1D = 32
B2D = 64
SLOT = 128
PAIRS = HEADS // 2
TAPS = 7
REACH = 3
EPSILON = 1e-05
MASKED = -1000000000.0
STRIP = 64

f32 = jnp.float32
bf16 = jnp.bfloat16
NN = ((1,), (0,))
NT = ((1,), (1,))
TN = ((0,), (0,))

IN_VMEM = pl.BlockSpec(memory_space=pltpu.VMEM)
IN_SMEM = pl.BlockSpec(memory_space=pltpu.SMEM)
IN_PLACE = pl.BlockSpec(memory_space=pl.ANY)


def dot(left, right, dims=NN, precision=None):
    return lax.dot_general(
        left, right, (dims, ((), ())), precision=precision, preferred_element_type=f32
    )


def iota(shape, axis):
    return lax.broadcasted_iota(jnp.int32, shape, axis)


def hot(mask):
    return mask.astype(f32).astype(bf16)


def identity():
    return hot(iota((SLOT, SLOT), 0) == iota((SLOT, SLOT), 1))


def rank_hot_of(order):
    return hot(order == iota((SLOT, SLOT), 0))


def page_hot(order, column, row):
    cells = iota((SLOT, SLOT), 0)
    wanted = jnp.where(cells < B2D, column, row + B2D)
    cell_hot = dot(identity(), hot(wanted == cells), NT).astype(bf16)
    return jnp.concatenate([rank_hot_of(order), cell_hot], axis=1)


def tap_columns(order, region, length):
    shape = (8, SLOT)
    order, region = jnp.broadcast_to(order, shape), jnp.broadcast_to(region, shape)
    live = (order < length).astype(jnp.int32)
    lane, tap = iota(shape, 1), iota(shape, 0)
    masks = jnp.zeros(shape, f32)
    for j in range(TAPS):
        offset = j - REACH
        shift = (-offset) % SLOT
        region_j = pltpu.roll(region, shift, 1) if shift else region
        live_j = pltpu.roll(live, shift, 1) if shift else live
        joined = (lane + offset >= 0) & (lane + offset < SLOT) & (region_j == region) & (live_j > 0)
        masks = jnp.where((tap == j) & joined, 1.0, masks)
    return dot(identity(), masks.astype(bf16), NT)


def shifted(rows, offset):
    shift = (-offset) % SLOT
    return pltpu.roll(rows, shift, 0) if shift else rows


def place_rows(rank_hot, rows, dims):
    high = rows.astype(bf16)
    low = (rows - high.astype(f32)).astype(bf16)
    return dot(rank_hot, high, dims) + dot(rank_hot, low, dims)


def bucket_places():
    shape = (B1D + 2 * B2D, 4 * SLOT)
    bucket, lane = iota(shape, 0), iota(shape, 1)
    near = jnp.clip(lane - (SLOT - 1) + B1D // 2, 0, B1D - 1)
    column = B1D + jnp.clip(lane - 2 * SLOT - (B2D - 1) + B2D // 2, 0, B2D - 1)
    row = B1D + B2D + jnp.clip(lane - 3 * SLOT - (B2D - 1) + B2D // 2, 0, B2D - 1)
    wanted = jnp.where(lane < 2 * SLOT, near, jnp.where(lane < 3 * SLOT, column, row))
    return bucket == wanted


def halves(pair):
    lane = iota((1, SLOT), 1)
    first = hot(lane < HEAD)
    second = hot(lane >= HEAD)
    return jnp.concatenate([pair * first, pair * second], axis=0)


def side_by_side(stacked):
    return jnp.concatenate([stacked[:SLOT], stacked[SLOT:]], axis=1)


def normed_of(value):
    average = jnp.mean(value, axis=-1, keepdims=True)
    centered = value - average
    spread = jnp.mean(centered * centered, axis=-1, keepdims=True)
    inverse = lax.rsqrt(spread + EPSILON)
    return centered * inverse, inverse


def norm_back(grad, normed, inverse):
    first_mean = jnp.mean(grad, axis=-1, keepdims=True)
    second_mean = jnp.mean(grad * normed, axis=-1, keepdims=True)
    return inverse * (grad - first_mean - normed * second_mean)


def copies_in(pairs, sems):
    copies = [pltpu.make_async_copy(a, b, sems.at[i]) for i, (a, b) in enumerate(pairs)]
    for copy in copies:
        copy.start()
    return copies


def bias_body(order_ref, column_ref, row_ref, table_ref, bias_ref):
    pages = order_ref.shape[0]
    hots = [
        page_hot(order_ref[p : p + 1, :], column_ref[p : p + 1, :], row_ref[p : p + 1, :])
        for p in range(pages)
    ]
    every = jnp.concatenate(hots, axis=0)
    reach = dot(table_ref[...], hot(bucket_places()), TN)
    lane = iota((B2D, SLOT), 1)
    for h in range(HEADS):
        row = reach[h : h + 1, :]
        near = jnp.broadcast_to(row[:, : 2 * SLOT], (SLOT, 2 * SLOT))
        near = pltpu.roll(near, SLOT + 1, 1, stride=1, stride_axis=0)[:, :SLOT]
        across = jnp.broadcast_to(row[:, 2 * SLOT : 3 * SLOT], (B2D, SLOT))
        across = pltpu.roll(across, B2D + 1, 1, stride=1, stride_axis=0)
        down = jnp.broadcast_to(row[:, 3 * SLOT :], (B2D, SLOT))
        down = pltpu.roll(down, 1, 1, stride=1, stride_axis=0)
        cells = jnp.concatenate(
            [jnp.where(lane < B2D, across, 0.0), jnp.where(lane >= B2D, down, 0.0)], axis=0
        )
        blank = jnp.zeros((SLOT, SLOT), bf16)
        grid = jnp.concatenate(
            [
                jnp.concatenate([near.astype(bf16), blank], axis=1),
                jnp.concatenate([blank, cells.astype(bf16)], axis=1),
            ],
            axis=0,
        )
        rows = dot(every, grid).astype(bf16)
        for p in range(pages):
            at = (p * HEADS + h) * SLOT
            bias_ref[at : at + SLOT, :] = dot(rows[p * SLOT : (p + 1) * SLOT], hots[p], NT)


def forward_body(weights, waits, lengths_ref, vectors, bias_ref, work, keep, done):
    input_ref, output_ref, up_ref, down_ref = weights
    rows_ref, gains_ref, up_bias_ref = vectors
    mixed_ref, packed_ref, attended_ref, sum_ref, first_ref, low_ref, act_ref, result_ref = work
    rows, gains = rows_ref[...].astype(f32), gains_ref[...].astype(f32)
    tokens, width = mixed_ref.shape
    hidden = act_ref.shape[1]
    low_ref[...] = mixed_ref[...].astype(bf16)
    if keep:
        keep["mixed_low"][...] = low_ref[...]
        done("mixed_low")
    waits[0]()
    for part, add in ((0, rows[0:1]), (1, None), (2, rows[1:2])):
        cols = slice(part * width, (part + 1) * width)
        value = dot(low_ref[...], input_ref[:, cols])
        packed_ref[:, cols] = (value if add is None else value + add).astype(bf16)
    if keep:
        done("packed")
    for p in range(tokens // SLOT):
        live = iota((2 * SLOT, SLOT), 1) < lengths_ref[p]
        here = slice(p * SLOT, (p + 1) * SLOT)
        for pair in range(PAIRS):
            at = pair * SLOT
            queries = halves(packed_ref[here, at : at + SLOT]) * (HEAD**-0.5)
            keys = packed_ref[here, width + at : width + at + SLOT]
            values = packed_ref[here, 2 * width + at : 2 * width + at + SLOT]
            top = (p * HEADS + 2 * pair) * SLOT
            scores = dot(queries, keys, NT) + bias_ref[top : top + 2 * SLOT, :]
            scores = jnp.where(live, scores, MASKED)
            expo = jnp.exp(scores - jnp.max(scores, axis=-1, keepdims=True))
            probs = (expo * (1.0 / jnp.sum(expo, axis=-1, keepdims=True))).astype(bf16)
            if keep:
                keep["probs"][top : top + 2 * SLOT, :] = probs
            attended_ref[here, at : at + SLOT] = dot(side_by_side(probs), halves(values)).astype(
                bf16
            )
    if keep:
        done("probs")
        done("attended")
    waits[1]()
    sum_ref[...] = dot(attended_ref[...], output_ref[...])
    for r in range(0, tokens, STRIP):
        strip = slice(r, r + STRIP)
        normed, inverse = normed_of(mixed_ref[strip] + sum_ref[strip] + rows[2:3])
        first = normed * gains[0:1] + rows[3:4]
        first_ref[strip] = first
        low_ref[strip] = first.astype(bf16)
        if keep:
            keep["first_norm"][strip] = normed
            keep["first_scale"][strip] = jnp.broadcast_to(inverse, (STRIP, SLOT))
            keep["first_low"][strip] = first.astype(bf16)
    if keep:
        done("first_norm")
        done("first_scale")
        done("first_low")
    waits[2]()
    for c in range(0, hidden, 2 * SLOT):
        cols = slice(c, c + 2 * SLOT)
        gate = dot(low_ref[...], up_ref[:, cols]) + up_bias_ref[:, cols].astype(f32)
        below = 0.5 + 0.5 * lax.erf(gate * 0.7071067811865476)
        act_ref[:, cols] = (gate * below).astype(bf16)
        if keep:
            density = jnp.exp(-0.5 * gate * gate) * 0.3989422804014327
            keep["slope"][:, cols] = (below + gate * density).astype(bf16)
    if keep:
        done("slope")
        done("act")
    waits[3]()
    sum_ref[...] = dot(act_ref[...], down_ref[...])
    for r in range(0, tokens, STRIP):
        strip = slice(r, r + STRIP)
        normed, inverse = normed_of(first_ref[strip] + sum_ref[strip] + rows[4:5])
        result_ref[strip] = (normed * gains[1:2] + rows[5:6]).astype(bf16)
        if keep:
            keep["second_norm"][strip] = normed
            keep["second_scale"][strip] = jnp.broadcast_to(inverse, (STRIP, SLOT))
    if keep:
        done("second_norm")
        done("second_scale")


def attention_back(p, pair, packed_ref, probs_ref, grad_ref, grad_packed_ref, width):
    here = slice(p * SLOT, (p + 1) * SLOT)
    at = pair * SLOT
    top = (p * HEADS + 2 * pair) * SLOT
    queries = halves(packed_ref[here, at : at + SLOT]) * (HEAD**-0.5)
    keys = halves(packed_ref[here, width + at : width + at + SLOT]) * (HEAD**-0.5)
    values = packed_ref[here, 2 * width + at : 2 * width + at + SLOT]
    grad = halves(grad_ref[here, at : at + SLOT])
    probs_low = probs_ref[top : top + 2 * SLOT, :]
    probs = probs_low.astype(f32)
    grad_probs = dot(grad, values, NT)
    inner = jnp.sum(probs * grad_probs, axis=-1, keepdims=True)
    grad_scores = (probs * (grad_probs - inner)).astype(bf16)
    for part, value in (
        (0, dot(side_by_side(grad_scores), keys)),
        (1, dot(grad_scores, queries, TN)),
        (2, dot(probs_low, grad, TN)),
    ):
        cols = slice(part * width + at, part * width + at + SLOT)
        grad_packed_ref[here, cols] = value.astype(bf16)
    return grad_scores


def first_kernel(
    tokens_ref,
    lengths_ref,
    flags_ref,
    order_ref,
    region_ref,
    column_ref,
    row_ref,
    rows_ref,
    gains_ref,
    up_bias_ref,
    taps_ref,
    table_ref,
    input_hbm,
    output_hbm,
    up_hbm,
    down_hbm,
    result_ref,
    mixed_ref,
    bias_ref,
    input_ref,
    output_ref,
    up_ref,
    down_ref,
    packed_ref,
    attended_ref,
    sum_ref,
    first_ref,
    low_ref,
    act_ref,
    sems,
):
    copies = copies_in(
        (
            (input_hbm, input_ref),
            (output_hbm, output_ref),
            (up_hbm, up_ref),
            (down_hbm, down_ref),
        ),
        sems,
    )
    conv_on = flags_ref[0].astype(f32)
    taps = taps_ref[...].astype(f32) * conv_on
    conv_bias = rows_ref[...].astype(f32)[6:7] * conv_on
    for p in range(order_ref.shape[0]):
        here = slice(p * SLOT, (p + 1) * SLOT)
        order = order_ref[p : p + 1, :]
        rank_hot = rank_hot_of(order)
        masks = tap_columns(order, region_ref[p : p + 1, :], lengths_ref[p])
        ordered = dot(rank_hot, tokens_ref[here], TN)
        total = jnp.zeros_like(ordered)
        for j in range(TAPS):
            total = total + taps[j : j + 1] * shifted(ordered, j - REACH) * masks[:, j : j + 1]
        mixed_ref[here] = (
            tokens_ref[here].astype(f32) + place_rows(rank_hot, total, NN) + conv_bias
        )
    bias_body(order_ref, column_ref, row_ref, table_ref, bias_ref)
    forward_body(
        (input_ref, output_ref, up_ref, down_ref),
        [copy.wait for copy in copies],
        lengths_ref,
        (rows_ref, gains_ref, up_bias_ref),
        bias_ref,
        (
            mixed_ref,
            packed_ref,
            attended_ref,
            sum_ref,
            first_ref,
            low_ref,
            act_ref,
            result_ref,
        ),
        None,
        None,
    )


KEPT = (
    ("mixed_low", 1, 0),
    ("packed", 3, 0),
    ("probs", 0, 0),
    ("attended", 1, 0),
    ("first_norm", 1, 1),
    ("first_scale", -1, 1),
    ("first_low", 1, 0),
    ("slope", 4, 0),
    ("act", 4, 0),
    ("second_norm", 1, 1),
    ("second_scale", -1, 1),
)


def kept_shapes(tokens, width, hidden):
    shapes = []
    for name, parts, wide in KEPT:
        dims = (tokens, hidden if parts == 4 else SLOT if parts < 0 else parts * width)
        if name == "probs":
            dims = (tokens * HEADS, SLOT)
        shapes.append((dims, f32 if wide else bf16))
    return shapes


def second_kernel(
    arrived_ref,
    cotangent_ref,
    lengths_ref,
    flags_ref,
    rows_ref,
    gains_ref,
    up_bias_ref,
    mixed_hbm,
    bias_hbm,
    input_hbm,
    output_hbm,
    up_hbm,
    down_hbm,
    result_ref,
    grad_in_ref,
    *rest,
):
    count = len(KEPT)
    kept_out, rest = rest[:count], rest[count:]
    kept_list, rest = rest[:count], rest[count:]
    (
        mixed_ref,
        bias_ref,
        input_ref,
        output_ref,
        up_ref,
        down_ref,
        sum_ref,
        first_ref,
        low_ref,
        gate_ref,
        grad_ref,
        grad_packed_ref,
        sems,
        kept_sems,
    ) = rest
    tokens, width = mixed_ref.shape
    hidden = gate_ref.shape[1]
    copies = copies_in(
        (
            (mixed_hbm, mixed_ref),
            (input_hbm, input_ref),
            (bias_hbm, bias_ref),
            (output_hbm, output_ref),
            (up_hbm, up_ref),
            (down_hbm, down_ref),
        ),
        sems,
    )
    names = [name for name, _, _ in KEPT]
    keep = dict(zip(names, kept_list))
    leaving = []

    def done(name):
        at = names.index(name)
        copy = pltpu.make_async_copy(kept_list[at], kept_out[at], kept_sems.at[at])
        copy.start()
        leaving.append(copy)

    copies[0].wait()
    first_section = flags_ref[0] > 0
    mixed_ref[...] = jnp.where(first_section, mixed_ref[...], arrived_ref[...].astype(f32))

    def wait_input():
        copies[1].wait()
        copies[2].wait()

    forward_body(
        (input_ref, output_ref, up_ref, down_ref),
        (wait_input, copies[3].wait, copies[4].wait, copies[5].wait),
        lengths_ref,
        (rows_ref, gains_ref, up_bias_ref),
        bias_ref,
        (
            mixed_ref,
            keep["packed"],
            keep["attended"],
            sum_ref,
            first_ref,
            low_ref,
            keep["act"],
            result_ref,
        ),
        keep,
        done,
    )
    gains = gains_ref[...].astype(f32)
    for r in range(0, tokens, STRIP):
        strip = slice(r, r + STRIP)
        grad = cotangent_ref[strip].astype(f32) * gains[1:2]
        grad_sum = norm_back(grad, keep["second_norm"][strip], keep["second_scale"][strip, :1])
        first_ref[strip] = grad_sum
        low_ref[strip] = grad_sum.astype(bf16)
    gate_body(low_ref, down_ref, keep["slope"], gate_ref)
    for c in range(0, width, 2 * SLOT):
        cols = slice(c, c + 2 * SLOT)
        sum_ref[:, cols] = first_ref[:, cols] + dot(gate_ref[...], up_ref[cols, :], NT)
    for r in range(0, tokens, STRIP):
        strip = slice(r, r + STRIP)
        grad = sum_ref[strip] * gains[0:1]
        grad_mid = norm_back(grad, keep["first_norm"][strip], keep["first_scale"][strip, :1])
        first_ref[strip] = grad_mid
        low_ref[strip] = grad_mid.astype(bf16)
    grad_ref[...] = dot(low_ref[...], output_ref[...], NT).astype(bf16)
    for p in range(tokens // SLOT):
        for pair in range(PAIRS):
            attention_back(
                p, pair, keep["packed"], keep["probs"], grad_ref, grad_packed_ref, width
            )
    for c in range(0, width, 2 * SLOT):
        cols = slice(c, c + 2 * SLOT)
        grad_in = first_ref[:, cols] + dot(grad_packed_ref[...], input_ref[cols, :], NT)
        grad_in_ref[:, cols] = grad_in.astype(bf16)
    for copy in leaving:
        copy.wait()


def gate_body(grad_ref, down_ref, slope_ref, gate_ref):
    for c in range(0, gate_ref.shape[1], 2 * SLOT):
        cols = slice(c, c + 2 * SLOT)
        value = dot(grad_ref[...], down_ref[cols, :], NT) * slope_ref[:, cols].astype(f32)
        gate_ref[:, cols] = value.astype(bf16)


class Shares:
    def __init__(self, held_ref, outs, core, sems):
        self.held, self.outs, self.core, self.sems = held_ref, outs, core, sems
        self.copies, self.sent = [], 0

    def rows_done(self, rows):
        if len(self.outs) == 1:
            if rows == self.held.shape[0]:
                self._start(self.held, self.outs[0])
            return
        share = self.outs[0].shape[1]
        while (self.sent + 1) * 2 * share <= rows:
            for out, parity in zip(self.outs, (1 - self.core, self.core)):
                start = pl.multiple_of((2 * self.sent + parity) * share, 16)
                self._start(self.held.at[pl.ds(start, share)], out.at[self.sent])
            self.sent += 1

    def _start(self, source, target):
        copy = pltpu.make_async_copy(source, target, self.sems.at[len(self.copies)])
        copy.start()
        self.copies.append(copy)

    def wait(self):
        for copy in self.copies:
            copy.wait()


def column_sum(value):
    return jnp.sum(value, axis=0, keepdims=True)


def down_kernel(
    cotangent_ref,
    arrived_ref,
    flags_ref,
    gains_ref,
    normed_ref,
    scale_ref,
    act_ref,
    *rest,
    outs,
):
    shares_out, (grad_sum_ref, small_ref, low_ref, held_ref, sems) = rest[:outs], rest[outs:]
    tokens = low_ref.shape[0]
    hidden = act_ref.shape[1]
    gains = gains_ref[...].astype(f32)
    last = flags_ref[2] > 0
    sums = [0.0, 0.0, 0.0]
    for r in range(0, tokens, STRIP):
        strip = slice(r, r + STRIP)
        grad_out = jnp.where(
            last, cotangent_ref[strip].astype(f32), arrived_ref[strip].astype(f32)
        )
        normed = normed_ref[strip]
        grad_sum = norm_back(grad_out * gains[1:2], normed, scale_ref[strip, :1])
        low = grad_sum.astype(bf16)
        grad_sum_ref[strip] = grad_sum
        low_ref[strip] = low
        sums[0] = sums[0] + column_sum(low.astype(f32))
        sums[1] = sums[1] + column_sum(grad_out)
        sums[2] = sums[2] + column_sum(grad_out * normed)
    shares = Shares(held_ref, shares_out, flags_ref[1], sems)
    step = 3 * SLOT
    for r in range(0, hidden, step):
        held_ref[r : r + step, :] = dot(act_ref[:, r : r + step], low_ref[...], TN).astype(bf16)
        shares.rows_done(r + step)
    for i, value in enumerate(sums):
        small_ref[i : i + 1, :] = value
    shares.wait()


def up_kernel(grad_sum_ref, flags_ref, slope_ref, first_low_ref, down_hbm, *rest, outs):
    shares_out, (gate_ref, small_ref, low_ref, down_ref, held_ref, sem, sems) = (
        rest[:outs],
        rest[outs:],
    )
    (copy,) = copies_in(((down_hbm, down_ref),), sem)
    low_ref[...] = grad_sum_ref[...].astype(bf16)
    copy.wait()
    gate_body(low_ref, down_ref, slope_ref, gate_ref)
    shares = Shares(held_ref, shares_out, flags_ref[1], sems)
    width, hidden = held_ref.shape
    step = 3 * SLOT
    for r in range(0, width, step):
        left = first_low_ref[:, r : r + step]
        for c in range(0, hidden, width):
            cols = slice(c, c + width)
            held_ref[r : r + step, cols] = dot(left, gate_ref[:, cols], TN).astype(bf16)
        shares.rows_done(r + step)
    for c in range(0, hidden, width):
        cols = slice(c, c + width)
        small_ref[:, cols] = column_sum(gate_ref[:, cols].astype(f32))
    shares.wait()


def backwards(every):
    shape = (2 * SLOT, 2 * SLOT)
    left, right = iota(shape, 0), iota(shape, 1)
    ends = jnp.where(left < SLOT, SLOT - 1, jnp.where(left < SLOT + B2D, 3 * SLOT - B2D - 1, 0))
    ends = jnp.where(left >= SLOT + B2D, 4 * SLOT - B2D - 1, ends)
    return dot(every, hot(left + right == ends)).astype(bf16)


def table_rows(sums):
    blank = jnp.zeros((SLOT, SLOT), f32)
    near = jnp.concatenate([sums[:SLOT, :SLOT], blank], axis=1)
    near = pltpu.roll(near, 0, 1, stride=1, stride_axis=0)
    lane = iota((B2D, SLOT), 1)
    across = jnp.where(lane < B2D, sums[SLOT : SLOT + B2D, SLOT:], 0.0)
    across = pltpu.roll(across, 0, 1, stride=1, stride_axis=0)
    down = jnp.where(lane >= B2D, sums[SLOT + B2D :, SLOT:], 0.0)
    down = pltpu.roll(down, B2D, 1, stride=1, stride_axis=0)
    return jnp.concatenate([column_sum(near), column_sum(across), column_sum(down)], axis=1)


def last_kernel(
    grad_sum_ref,
    gate_ref,
    normed_ref,
    scale_ref,
    attended_ref,
    packed_ref,
    probs_ref,
    mixed_low_ref,
    tokens_ref,
    small_down_ref,
    lengths_ref,
    flags_ref,
    order_ref,
    region_ref,
    column_ref,
    row_ref,
    gains_ref,
    taps_ref,
    up_hbm,
    output_hbm,
    input_hbm,
    *rest,
    outs,
):
    shares_out, rest = rest[:outs], rest[outs:]
    grad_in_ref, small_ref, table_ref, rest = rest[0], rest[1], rest[2], rest[3:]
    (
        up_ref,
        output_ref,
        input_ref,
        sum_ref,
        mid_ref,
        low_ref,
        grad_ref,
        grad_packed_ref,
        reach_ref,
        held_ref,
        weight_sems,
        sems,
    ) = rest
    copies = copies_in(
        ((up_hbm, up_ref), (output_hbm, output_ref), (input_hbm, input_ref)), weight_sems
    )
    tokens, width = sum_ref.shape
    pages = tokens // SLOT
    conv_on = flags_ref[0].astype(f32)
    gains = gains_ref[...].astype(f32)
    taps = taps_ref[...].astype(f32) * conv_on
    copies[0].wait()
    for c in range(0, width, 2 * SLOT):
        cols = slice(c, c + 2 * SLOT)
        sum_ref[:, cols] = grad_sum_ref[:, cols] + dot(gate_ref[...], up_ref[cols, :], NT)
    first_sum = gain_sum = branch_sum = 0.0
    for r in range(0, tokens, STRIP):
        strip = slice(r, r + STRIP)
        grad_first, normed = sum_ref[strip], normed_ref[strip]
        grad_mid = norm_back(grad_first * gains[0:1], normed, scale_ref[strip, :1])
        low = grad_mid.astype(bf16)
        mid_ref[strip] = grad_mid
        low_ref[strip] = low
        first_sum = first_sum + column_sum(grad_first)
        gain_sum = gain_sum + column_sum(grad_first * normed)
        branch_sum = branch_sum + column_sum(low.astype(f32))
    copies[1].wait()
    grad_ref[...] = dot(low_ref[...], output_ref[...], NT).astype(bf16)
    hots = [
        page_hot(order_ref[p : p + 1, :], column_ref[p : p + 1, :], row_ref[p : p + 1, :])
        for p in range(pages)
    ]
    every = backwards(jnp.concatenate(hots, axis=0))
    reach_ref[...] = jnp.zeros_like(reach_ref)
    for pair in range(PAIRS):
        scores = [
            attention_back(p, pair, packed_ref, probs_ref, grad_ref, grad_packed_ref, width)
            for p in range(pages)
        ]
        for head in range(2):
            rows = slice(head * SLOT, (head + 1) * SLOT)
            along = jnp.concatenate([dot(s[rows], h) for s, h in zip(scores, hots)], axis=0)
            sums = dot(every, along.astype(bf16), TN)
            at = 2 * pair + head
            reach_ref[at : at + 1, :] = table_rows(sums)
    shares = Shares(held_ref, shares_out, flags_ref[1], sems)
    step = 3 * SLOT
    for r in range(0, width, step):
        rows = slice(r, r + step)
        held_ref[rows, :width] = dot(attended_ref[:, rows], low_ref[...], TN).astype(bf16)
        for c in range(0, 3 * width, width):
            value = dot(mixed_low_ref[:, rows], grad_packed_ref[:, c : c + width], TN)
            held_ref[rows, width + c : 2 * width + c] = value.astype(bf16)
        shares.rows_done(r + step)
    copies[2].wait()
    for c in range(0, width, 2 * SLOT):
        cols = slice(c, c + 2 * SLOT)
        sum_ref[:, cols] = mid_ref[:, cols] + dot(grad_packed_ref[...], input_ref[cols, :], NT)
    tap_sums = [0.0] * TAPS
    mixed_sum = 0.0
    for p in range(pages):
        here = slice(p * SLOT, (p + 1) * SLOT)
        order = order_ref[p : p + 1, :]
        rank_hot = rank_hot_of(order)
        masks = tap_columns(order, region_ref[p : p + 1, :], lengths_ref[p])
        ordered = dot(rank_hot, tokens_ref[here], TN)
        grad_mixed = sum_ref[here]
        grad_order = place_rows(rank_hot, grad_mixed, TN)
        source = jnp.zeros_like(ordered)
        for j in range(TAPS):
            masked = grad_order * masks[:, j : j + 1]
            tap_sums[j] = tap_sums[j] + column_sum(masked * shifted(ordered, j - REACH))
            source = source + shifted(taps[j : j + 1] * masked, REACH - j)
        grad_in_ref[here] = grad_mixed + place_rows(rank_hot, source, NN)
        mixed_sum = mixed_sum + column_sum(grad_mixed)
    small_down = small_down_ref[...]
    rows = [
        column_sum(grad_packed_ref[:, :width].astype(f32)),
        column_sum(grad_packed_ref[:, 2 * width :].astype(f32)),
        branch_sum,
        first_sum,
        small_down[0:1],
        small_down[1:2],
        conv_on * mixed_sum,
        gain_sum,
        small_down[2:3],
    ]
    for i, value in enumerate(rows + [conv_on * value for value in tap_sums]):
        small_ref[i : i + 1, :] = value
    table_ref[...] = dot(
        bucket_places().astype(f32), reach_ref[...], NT, precision=lax.Precision.HIGHEST
    )
    shares.wait()


def kernel_call(body, name, ins, outs, scratch, flops):
    nbytes = sum(value.size * value.dtype.itemsize for value, _ in list(ins) + list(outs))
    return pl.pallas_call(
        body,
        name=name,
        out_shape=[shape for shape, _ in outs],
        in_specs=[spec for _, spec in ins],
        out_specs=[spec for _, spec in outs],
        scratch_shapes=scratch,
        compiler_params=pltpu.CompilerParams(vmem_limit_bytes=56 << 20),
        cost_estimate=pl.CostEstimate(flops=int(flops), bytes_accessed=nbytes, transcendentals=0),
    )(*[value for value, _ in ins])


def taken(value, index, axis):
    return lax.dynamic_index_in_dim(value, index, axis, keepdims=False).astype(f32)


def summed(theirs, mine):
    index = lax.axis_index("dp")
    z, y = index // 4, (index // 2) % 2
    everyone = range(16)

    def swapped(value, bits):
        return lax.ppermute(value, "dp", [(i, i ^ bits) for i in everyone])

    theirs, mine = (v.reshape((4, 2) + v.shape[1:]) for v in (theirs, mine))
    core_part = swapped(theirs, 1)
    leaving = (taken(mine, 1 - y, 1) + taken(core_part, 1 - y, 1)).astype(bf16)
    y_part = swapped(leaving, 2)
    kept = taken(mine, y, 1) + taken(core_part, y, 1) + y_part.astype(f32)
    kept = kept.astype(bf16)
    total = taken(kept, z, 0)
    for step in (1, 2, 3):
        part = lax.dynamic_index_in_dim(kept, z ^ step, 0, keepdims=False)
        total = total + swapped(part, 4 * step).astype(f32)
    return total


def local(
    tokens,
    cotangent,
    page_lengths,
    cut_order,
    cut_region,
    cell_column,
    cell_row,
    input_proj,
    output_proj,
    up_proj,
    down_proj,
    up_bias,
    bias_rows,
    gain_rows,
    conv_taps,
    bias_table,
):
    section_index = lax.axis_index("section")
    section_count = lax.axis_size("section")
    dp_index = lax.axis_index("dp")
    dp_count = lax.axis_size("dp")
    by_hops = dp_count == 16
    pages, _, width = tokens.shape
    hidden = up_proj.shape[2]
    count = pages * SLOT
    weights = [w[0] for w in (input_proj, output_proj, up_proj, down_proj)]
    input_w, output_w, up_w, down_w = weights
    rows, gains, taps = bias_rows[0], gain_rows[0], conv_taps[0]
    table = jnp.pad(bias_table[0].reshape(-1, HEADS), ((0, 0), (0, 16 - HEADS)))
    flags = jnp.stack(
        [
            (section_index == 0).astype(jnp.int32),
            (dp_index % 2).astype(jnp.int32),
            (section_index == section_count - 1).astype(jnp.int32),
        ]
    )
    tokens, cotangent = tokens.reshape(count, width), cotangent.reshape(count, width)
    work = 2 * count * (4 * width * width + 2 * width * hidden)

    def shape(dims, kind):
        return jax.ShapeDtypeStruct(dims, kind)

    def inside(*values):
        return [(v, IN_VMEM) for v in values]

    def in_place(*values):
        return [(v, IN_PLACE) for v in values]

    def scalars(*values):
        return [(v, IN_SMEM) for v in values]

    wide, low = shape((count, width), f32), shape((count, width), bf16)
    weight_scratch = [pltpu.VMEM(w.shape, w.dtype) for w in weights]
    wide_scratch = pltpu.VMEM((count, width), f32)
    low_scratch = pltpu.VMEM((count, width), bf16)
    packed_scratch = pltpu.VMEM((count, 3 * width), bf16)
    hidden_scratch = pltpu.VMEM((count, hidden), bf16)
    bias_dims = (pages * HEADS * SLOT, SLOT)

    def sems(number):
        return pltpu.SemaphoreType.DMA((number,))

    result, mixed, bias = kernel_call(
        first_kernel,
        "first",
        inside(tokens)
        + scalars(page_lengths, flags)
        + inside(cut_order, cut_region, cell_column, cell_row, rows, gains, up_bias, taps, table)
        + in_place(*weights),
        inside(low, wide, shape(bias_dims, f32)),
        weight_scratch
        + [
            packed_scratch,
            low_scratch,
            wide_scratch,
            wide_scratch,
            low_scratch,
            hidden_scratch,
            sems(4),
        ],
        work,
    )
    arrived = lax.ppermute(result, "section", [(i, i + 1) for i in range(section_count - 1)])
    shapes = kept_shapes(count, width, hidden)
    layer_out, leaving, *kept_list = kernel_call(
        second_kernel,
        "second",
        inside(arrived, cotangent)
        + scalars(page_lengths, flags)
        + inside(rows, gains, up_bias)
        + in_place(mixed, bias, *weights),
        inside(low, low) + in_place(*[shape(*s) for s in shapes]),
        [pltpu.VMEM(*s) for s in shapes]
        + [wide_scratch, pltpu.VMEM(bias_dims, f32)]
        + weight_scratch
        + [
            wide_scratch,
            wide_scratch,
            low_scratch,
            hidden_scratch,
            low_scratch,
            packed_scratch,
            sems(6),
            sems(len(KEPT)),
        ],
        2 * work,
    )
    kept = dict(zip([name for name, _, _ in KEPT], kept_list))
    arrived_grad = lax.ppermute(
        leaving, "section", [(i + 1, i) for i in range(section_count - 1)]
    )

    def share_outs(dims):
        if not by_hops:
            return in_place(shape(dims, bf16))
        half = shape((dp_count // 2, dims[0] // dp_count, dims[1]), bf16)
        return in_place(half, half)

    def over_devices(parts):
        if by_hops:
            return summed(*parts)
        return lax.psum_scatter(parts[0], "dp", scatter_dimension=0, tiled=True).astype(f32)

    outs = 2 if by_hops else 1
    share_sems = sems(dp_count if by_hops else 1)
    *down_parts, grad_sum, small_down = kernel_call(
        functools.partial(down_kernel, outs=outs),
        "down",
        inside(cotangent, arrived_grad)
        + scalars(flags)
        + inside(gains, kept["second_norm"], kept["second_scale"], kept["act"]),
        share_outs((hidden, width)) + inside(wide, shape((8, width), f32)),
        [low_scratch, pltpu.VMEM((hidden, width), bf16), share_sems],
        2 * count * width * hidden,
    )
    *up_parts, gate, small_up = kernel_call(
        functools.partial(up_kernel, outs=outs),
        "up",
        inside(grad_sum)
        + scalars(flags)
        + inside(kept["slope"], kept["first_low"])
        + in_place(down_w),
        share_outs((width, hidden)) + inside(shape((count, hidden), bf16), shape((1, hidden), f32)),
        [
            low_scratch,
            weight_scratch[3],
            pltpu.VMEM((width, hidden), bf16),
            sems(1),
            share_sems,
        ],
        4 * count * width * hidden,
    )
    *in_parts, grad_in, small_rows, small_table = kernel_call(
        functools.partial(last_kernel, outs=outs),
        "last",
        inside(
            grad_sum,
            gate,
            kept["first_norm"],
            kept["first_scale"],
            kept["attended"],
            kept["packed"],
            kept["probs"],
            kept["mixed_low"],
            tokens,
            small_down,
        )
        + scalars(page_lengths, flags)
        + inside(cut_order, cut_region, cell_column, cell_row, gains, taps)
        + in_place(up_w, output_w, input_w),
        share_outs((width, 4 * width))
        + inside(wide, shape((16, width), f32), shape((B1D + 2 * B2D, 16), f32)),
        [
            weight_scratch[2],
            weight_scratch[1],
            weight_scratch[0],
            wide_scratch,
            wide_scratch,
            low_scratch,
            low_scratch,
            packed_scratch,
            pltpu.VMEM((16, 4 * SLOT), f32),
            pltpu.VMEM((width, 4 * width), bf16),
            sems(3),
            share_sems,
        ],
        3 * work,
    )
    down_grad = over_devices(down_parts)
    up_grad = over_devices(up_parts)
    in_grad = over_devices(in_parts)
    part = width // dp_count
    small = jnp.concatenate(
        [
            small_rows.reshape(16, dp_count, part).transpose(1, 0, 2).reshape(dp_count, -1),
            small_up.reshape(dp_count, -1),
            small_table[:, :HEADS].reshape(dp_count, -1),
        ],
        axis=1,
    )
    used = small.shape[1]
    small = jnp.pad(small, ((0, 0), (0, -used % SLOT))).reshape(-1, SLOT)
    small = lax.psum_scatter(small, "dp", scatter_dimension=0, tiled=True).reshape(-1)
    small_rows = small[: 16 * part].reshape(16, part)
    up_bias_grad = small[16 * part : 16 * part + hidden // dp_count]
    table_grad = small[16 * part + hidden // dp_count : used]
    return tuple(
        value[None]
        for value in (
            layer_out.reshape(pages, SLOT, width),
            grad_in.reshape(pages, SLOT, width),
            in_grad[:, width:],
            in_grad[:, :width],
            up_grad,
            down_grad,
            up_bias_grad,
            small_rows[:7],
            small_rows[7:9],
            small_rows[9:],
            table_grad,
        )
    )


def solution(mesh):
    by_section = [P("section", None, None)] * 4
    placed = (
        P("dp", None, None),
        P("dp", None, None),
        P("dp"),
        P("dp", None),
        P("dp", None),
        P("dp", None),
        P("dp", None),
        *by_section,
        P("section", None),
        P("section", None, None),
        P("section", None, None),
        P("section", None, None),
        P("section", None),
    )
    return jax.shard_map(
        local,
        mesh=mesh,
        in_specs=placed,
        out_specs=(
            P("section", "dp", None, None),
            P("section", "dp", None, None),
            P("section", "dp", None),
            P("section", "dp", None),
            P("section", "dp", None),
            P("section", "dp", None),
            P("section", "dp"),
            P("section", None, "dp"),
            P("section", None, "dp"),
            P("section", None, "dp"),
            P("section", "dp"),
        ),
        check_vma=False,
    )
```

time: 1180 us -> 354 us (0.30)
  waiting for transfers between devices: 642 us -> 205 us
  local copies, waits for them, and re-layouts: 179 us -> 18.8 us
  matrix products: 143 us -> 0 us
  other arithmetic: 99.9 us -> 12.2 us
  Pallas kernels: 0 us -> 70 us
  blocking collectives: 57.8 us -> 0 us
    reduce_scatter x4 -> x0, waiting for transfers between devices: 391 us -> none  [the longest x1 116 us: local(): lax.psum_scatter(totals[2], 'dp', scatter_dimension=0, tiled=True)]
    dot_general x62 -> x0, matrix products: 143 us -> none  [the longest x2 18 us: weight_terms(): jnp.einsum('sf,sd->fd', activated, grad_second, preferred_element_type=jn...]
    pallas_call x0 -> x5, Pallas kernels: none -> 70 us  [kernel_call(): pl.pallas_call(body, name=name, out_shape=[shape for shape, _ in outs], i...]
    unnamed x1 -> x0, blocking collectives: 57.8 us -> none
    another operation x66 -> x1, local copies, waits for them, and re-layouts: 48.9 us -> 0.13 us  [local(): table = jnp.pad(bias_table[0].reshape(-1, HEADS), ((0, 0), (0, 16 - HEADS)))]
    dynamic_update_slice x19 -> x0, other arithmetic: 27.4 us -> none  [the longest x15 21.7 us: place(): lax.dynamic_update_index_in_dim(stacked, element, position, 0)]
    ppermute x4 -> x17, waiting for transfers between devices: 146 us -> 120 us  [the longest x15 101 us: swapped(): return lax.ppermute(value, 'dp', [(i, i ^ bits) for i in everyone])]
    unnamed x10 -> x2, waiting for transfers between devices: 105 us -> 84.6 us
  transfers between devices with their start and end apart: 11 -> 18, of which waited for: 10 -> 9; matrix products, arithmetic and copies ran while one was open for 1% -> 7% of each run, Pallas kernels for 0% -> 9%
where the time goes in v1:
time: 354 us; the launch traced here: 347 us
  waiting for transfers between devices  205 us (58%)
  Pallas kernels  70 us (20%)
  starting transfers between devices  26 us (7%)
  local copies, waits for them, and re-layouts  18.8 us (5%)
  between operations  15.5 us (4%)
  other arithmetic  12.2 us (3%)
    ppermute x15, waiting for transfers between devices, swapped(): return lax.ppermute(value, 'dp', [(i, i ^ bits) for i in everyone])  101 us
    unnamed x2, waiting for transfers between devices  84.6 us
    pallas_call x5, Pallas kernels, kernel_call(): pl.pallas_call(body, name=name, out_shape=[shape for shape, _ in outs], i...  70 us
    ppermute x15, starting transfers between devices, swapped(): return lax.ppermute(value, 'dp', [(i, i ^ bits) for i in everyone])  19.7 us
    ppermute x1, waiting for transfers between devices, local(): lax.ppermute(leaving, 'section', [(i + 1, i) for i in range(section_count...  10.8 us
    ppermute x1, waiting for transfers between devices, local(): lax.ppermute(result, 'section', [(i, i + 1) for i in range(section_count...  8.47 us
    reshape x3, local copies, waits for them, and re-layouts, summed(): theirs, mine = (v.reshape((4, 2) + v.shape[1:]) for v in (theirs, mine))  8.29 us
  transfers between devices with their start and end apart: 18, of which 9 were waited for; matrix products, arithmetic and copies ran while one was open for 7% of the time, Pallas kernels for 9%

profile of v1, /device:TPU:0, one launch (start us, length us, event | category | flops | bytes accessed | tf_op | source)
XLA Modules:
  0.0 347.3 jit_solution(7636862870956055325)
XLA Ops:
  7.2 0.7 reduce
  8.1 0.6 pad.8.table_ref
  8.7 0.6 pad_add_fusion.flags_ref
  9.3 11.8 %first.1 = (bf16[256,768]{1,0:T(8,128)(2,1)}, f32[256,768]{1,0:T(8,128)}, f32[3072,128]{1,0:T(8,128)}) custom-call(bf16[256,768]{1,0:T(8,128)(2,1)} %bitcast.119, s32[2]{0:T(128)} %lengths_ref.5, s32[3]{0:T(128)} %pad_add_fusion.flags_ref, s32[2,128]{1,0:T(2,128)} %order_ref.3, s32[2,128]{1,0:T(2,128)} %region_ref.3, s32[2,128]{1,0:T(2,128)} %column_ref.3, ...), custom_call_target="tpu_custom_call" | custom-call | flops 3623878656 | bytes 17341460 | tf_op jit(solution)/shard_map/first/pallas_call | solution.py:747
  21.2 5.0 %collective-permute-start = (bf16[256,768]{1,0:T(8,128)(2,1)}, bf16[256,768]{1,0:T(8,128)(2,1)S(1)}, u32[]{:S(2)}, u32[]{:S(2)}) collective-permute-start(bf16[256,768]{1,0:T(8,128)(2,1)} %get-tuple-element.40), channel_id=1, source_target_pairs={{0,16},{1,17},{2,18},{3,19},{4,20},{5,21},{6,22},{7,23},{8,24},{9,... | collective-permute-start | bytes 1179656 | tf_op jit(solution)/shard_map/ppermute | solution.py:867
  26.2 8.5 %collective-permute-done.arrived_ref = bf16[256,768]{1,0:T(8,128)(2,1)S(1)} collective-permute-done((bf16[256,768]{1,0:T(8,128)(2,1)}, bf16[256,768]{1,0:T(8,128)(2,1)S(1)}, u32[]{:S(2)}, u32[]{:S(2)}) %collective-permute-start) | collective-permute-done | bytes 393248 | tf_op jit(solution)/shard_map/ppermute | solution.py:867
  34.7 0.7 copy-done.7
  35.4 22.3 %second.1 = (bf16[256,768]{1,0:T(8,128)(2,1)}, bf16[256,768]{1,0:T(8,128)(2,1)}, bf16[256,768]{1,0:T(8,128)(2,1)}, bf16[256,2304]{1,0:T(8,128)(2,1)}, bf16[3072,...) custom-call(bf16[256,768]{1,0:T(8,128)(2,1)} %copy-done.7, ...), custom_call_target="tpu_custom_call" | custom-call | flops 7247757312 | bytes 26234388 | tf_op jit(solution)/shard_map/second/pallas_call | solution.py:747
  57.7 1.3 collective-permute-start.1
  59.0 10.8 %collective-permute-done.1.arrived_ref = bf16[256,768]{1,0:T(8,128)(2,1)S(1)} collective-permute-done((bf16[256,768]{1,0:T(8,128)(2,1)}, bf16[256,768]{1,0:T(8,128)(2,1)S(1)}, u32[]{:S(2)}, u32[]{:S(2)}) %collective-permute-start.1) | collective-permute-done | bytes 393248 | tf_op jit(solution)/shard_map/ppermute | solution.py:893
  69.8 0.7 copy-done.8
  70.6 6.2 %down.1 = (bf16[8,192,768]{2,1,0:T(8,128)(2,1)}, bf16[8,192,768]{2,1,0:T(8,128)(2,1)}, f32[256,768]{1,0:T(8,128)}, f32[8,768]{1,0:T(8,128)}) custom-call(bf16[256,768]{1,0:T(8,128)(2,1)} %bitcast.132, bf16[256,768]{1,0:T(8,128)(2,1)} %copy-done.8, s32[3]{0:T(128)} %pad_add_fusion.flags_ref, bf16[2,768]{1,0:T(2,128)(2,1)} %bitcast.128, ...), custom_call_target="tpu_custom_call" | custom-call | flops 1207959552 | bytes 8809484 | tf_op jit(solution)/shard_map/down/pallas_call | solution.py:747
  76.7 3.3 copy.53
  80.0 9.6 %up.1 = (bf16[8,48,3072]{2,1,0:T(8,128)(2,1)}, bf16[8,48,3072]{2,1,0:T(8,128)(2,1)}, bf16[256,3072]{1,0:T(8,128)(2,1)}, f32[1,3072]{1,0:T(1,128)}) custom-call(f32[256,768]{1,0:T(8,128)} %get-tuple-element.48.grad_sum_ref, s32[3]{0:T(128)} %pad_add_fusion.flags_ref, bf16[256,3072]{1,0:T(8,128)(2,1)} %get-tuple-element.49.slope_ref, ...), custom_call_target="tpu_custom_call" | custom-call | flops 2415919104 | bytes 13774860 | tf_op jit(solution)/shard_map/up/pallas_call | solution.py:747
  89.7 20.0 %last.1 = (bf16[8,48,3072]{2,1,0:T(8,128)(2,1)}, bf16[8,48,3072]{2,1,0:T(8,128)(2,1)}, f32[256,768]{1,0:T(8,128)}, f32[16,768]{1,0:T(8,128)}, f32[160,16]{1,0:T(8,128)}) custom-call(f32[256,768]{1,0:T(8,128)} %get-tuple-element.48.grad_sum_ref, bf16[256,3072]{1,0:T(8,128)(2,1)} %get-tuple-element.51.gate_ref, f32[256,768]{1,0:T(8,128)} %get-tuple-element.52.normed_ref, ...), custom_call_target="tpu_custom_call" | custom-call | flops 10871635968 | bytes 21466644 | tf_op jit(solution)/shard_map/last/pallas_call | solution.py:747
  109.7 3.4 copy.47
  113.7 1.6 copy.50
  115.9 0.7 reduce.4
  117.0 0.6 reshape.108
  117.8 0.6 dynamic-slice
  119.0 84.5 %all-reduce.5.cloned.1.call-done = f32[144,128]{1,0:T(8,128)} async-done(((f32[144,128]{1,0:T(8,128)}), f32[144,128]{1,0:T(8,128)}) %all-reduce.5.cloned.1.call-update) | async-done | bytes 73744
  203.5 0.7 dynamic-slice_bitcast_fusion.9
  204.8 0.7 constant_dynamic-slice_fusion
  206.8 1.9 fusion.5
  208.7 1.0 collective-permute-start.13
  209.7 1.7 fusion.3
  211.4 1.2 collective-permute-start.3
  214.1 1.0 collective-permute-start.8
  215.1 22.6 %collective-permute-done.13 = bf16[4,192,768]{2,1,0:T(8,128)(2,1)S(1)} collective-permute-done((bf16[4,192,768]{2,1,0:T(8,128)(2,1)S(1)}, bf16[4,192,768]{2,1,0:T(8,128)(2,1)S(1)}, u32[]{:S(2)}, u32[]{:S(2)}) %collective-permute-start.13) | collective-permute-done | bytes 1179680 | tf_op jit(solution)/shard_map/ppermute | solution.py:769
  237.7 1.8 fusion
  239.5 3.4 collective-permute-start.14
  242.8 1.4 collective-permute-start.16
  244.3 18.7 %collective-permute-done.3 = bf16[4,48,3072]{2,1,0:T(8,128)(2,1)S(1)} collective-permute-done((bf16[4,48,3072]{2,1,0:T(8,128)(2,1)S(1)}, bf16[4,48,3072]{2,1,0:T(8,128)(2,1)S(1)}, u32[]{:S(2)}, u32[]{:S(2)}) %collective-permute-start.3) | collective-permute-done | bytes 1179680 | tf_op jit(solution)/shard_map/ppermute | solution.py:769
  262.9 1.8 fusion.2
  264.9 3.4 collective-permute-start.4
  268.2 1.4 collective-permute-start.6
  269.7 17.1 %collective-permute-done.8 = bf16[4,48,3072]{2,1,0:T(8,128)(2,1)S(1)} collective-permute-done((bf16[4,48,3072]{2,1,0:T(8,128)(2,1)S(1)}, bf16[4,48,3072]{2,1,0:T(8,128)(2,1)S(1)}, u32[]{:S(2)}, u32[]{:S(2)}) %collective-permute-start.8) | collective-permute-done | bytes 1179680 | tf_op jit(solution)/shard_map/ppermute | solution.py:769
  286.7 1.8 collective-permute-start.5
  289.2 1.2 collective-permute-start.15
  290.4 1.8 collective-permute-start.9
  292.1 15.4 %collective-permute-done.5 = bf16[48,3072]{1,0:T(8,128)(2,1)S(1)} collective-permute-done((bf16[48,3072]{1,0:T(8,128)(2,1)S(1)}, bf16[48,3072]{1,0:T(8,128)(2,1)S(1)}, u32[]{:S(2)}, u32[]{:S(2)}) %collective-permute-start.5) | collective-permute-done | bytes 294944 | tf_op jit(solution)/shard_map/ppermute | solution.py:769
  307.5 1.7 collective-permute-start.11
  309.3 0.8 slice_bitcast_fusion
  310.1 0.7 slice_bitcast_fusion.1
  310.8 15.7 %collective-permute-done.15 = bf16[192,768]{1,0:T(8,128)(2,1)S(1)} collective-permute-done((bf16[192,768]{1,0:T(8,128)(2,1)S(1)}, bf16[192,768]{1,0:T(8,128)(2,1)S(1)}, u32[]{:S(2)}, u32[]{:S(2)}) %collective-permute-start.15) | collective-permute-done | bytes 294944 | tf_op jit(solution)/shard_map/ppermute | solution.py:769
  326.5 1.0 fusion.8
  327.4 11.6 %collective-permute-done.10 = bf16[48,3072]{1,0:T(8,128)(2,1)S(1)} collective-permute-done((bf16[48,3072]{1,0:T(8,128)(2,1)S(1)}, bf16[48,3072]{1,0:T(8,128)(2,1)S(1)}, u32[]{:S(2)}, u32[]{:S(2)}) %collective-permute-start.10) | collective-permute-done | bytes 294944 | tf_op jit(solution)/shard_map/ppermute | solution.py:769
  339.0 1.0 fusion.11
  (55 shorter events, 6.1 us)
Async XLA Ops:
  7.2 196.4 %all-reduce.5.cloned.1.call-start = ((), (), s32[]{:S(2)}) async-start(), calls=%async_computation | async-start | bytes 147456
  21.2 13.5 %collective-permute-start = (bf16[256,768]{1,0:T(8,128)(2,1)}, bf16[256,768]{1,0:T(8,128)(2,1)S(1)}, u32[]{:S(2)}, u32[]{:S(2)}) collective-permute-start(bf16[256,768]{1,0:T(8,128)(2,1)} %get-tuple-element.40), channel_id=1, source_target_pairs={{0,16},{1,17},{2,18},{3,19},{4,20},{5,21},{6,22},{7,23},{8,24},{9,... | collective-permute-start | bytes 1179656 | tf_op jit(solution)/shard_map/ppermute | solution.py:867
  34.7 0.7 copy-start.7
  57.7 12.1 %collective-permute-start.1 = (bf16[256,768]{1,0:T(8,128)(2,1)}, bf16[256,768]{1,0:T(8,128)(2,1)S(1)}, u32[]{:S(2)}, u32[]{:S(2)}) collective-permute-start(bf16[256,768]{1,0:T(8,128)(2,1)} %get-tuple-element.44), channel_id=1, source_target_pairs={{16,0},{17,1},{18,2},{19,3},{20,4},{21,5},{22,6},{23,7},{24,8},{25... | collective-permute-start | bytes 1179656 | tf_op jit(solution)/shard_map/ppermute | solution.py:893
  69.8 0.7 copy-start.8
  80.0 126.8 %collective-permute-start.12 = (bf16[4,2,192,768]{3,2,0,1:T(8,128)(2,1)}, bf16[4,2,192,768]{3,2,0,1:T(8,128)(2,1)}, u32[]{:S(2)}, u32[]{:S(2)}) collective-permute-start(bf16[4,2,192,768]{3,2,0,1:T(8,128)(2,1)} %copy.53), channel_id=1, source_target_pairs={{0,1},{1,0},{2,3},{3,2},{4,5},{5,4},{6,7},{7,6},{8,9},{9,8},{10,11... | collective-permute-start | bytes 7077896 | tf_op jit(solution)/shard_map/ppermute | solution.py:769
  109.7 3.9 %copy-start.3 = (bf16[8,48,3072]{2,1,0:T(8,128)(2,1)S(1)}, bf16[8,48,3072]{2,1,0:T(8,128)(2,1)}, u32[]{:S(2)}) copy-start(bf16[8,48,3072]{2,1,0:T(8,128)(2,1)} %get-tuple-element.63) | copy-start | bytes 7077892
  113.1 96.6 %collective-permute-start.2 = (bf16[4,2,48,3072]{3,2,0,1:T(8,128)(2,1)}, bf16[4,2,48,3072]{3,2,0,1:T(8,128)(2,1)}, u32[]{:S(2)}, u32[]{:S(2)}) collective-permute-start(bf16[4,2,48,3072]{3,2,0,1:T(8,128)(2,1)} %copy.47), channel_id=1, source_target_pairs={{0,1},{1,0},{2,3},{3,2},{4,5},{5,4},{6,7},{7,6},{8,9},{9,8},{10,11... | collective-permute-start | bytes 7077896 | tf_op jit(solution)/shard_map/ppermute | solution.py:769
  113.6 1.7 copy-start.4
  113.6 2.3 copy-start.6
  113.6 3.0 copy-start.5
  113.6 4.1 %copy-start.9 = (u32[32]{0:T(128)S(1)}, u32[32]{0:T(128)}, u32[]{:S(2)}) copy-start(u32[32]{0:T(128)} %constant.146) | copy-start | bytes 388
  115.3 98.4 %collective-permute-start.7 = (bf16[4,2,48,3072]{3,2,0,1:T(8,128)(2,1)}, bf16[4,2,48,3072]{3,2,0,1:T(8,128)(2,1)S(1)}, u32[]{:S(2)}, u32[]{:S(2)}) collective-permute-start(bf16[4,2,48,3072]{3,2,0,1:T(8,128)(2,1)} %copy.50), channel_id=1, source_target_pairs={{0,1},{1,0},{2,3},{3,2},{4,5},{5,4},{6,7},{7,6},{8,9},{9,8},{10,11... | collective-permute-start | bytes 7077896 | tf_op jit(solution)/shard_map/ppermute | solution.py:769
  205.6 4.1 %copy-start.2 = (bf16[8,48,3072]{2,1,0:T(8,128)(2,1)S(1)}, bf16[8,48,3072]{2,1,0:T(8,128)(2,1)}, u32[]{:S(2)}) copy-start(bf16[8,48,3072]{2,1,0:T(8,128)(2,1)} %get-tuple-element.60) | copy-start | bytes 7077892
  208.7 5.0 %copy-start = (bf16[8,48,3072]{2,1,0:T(8,128)(2,1)S(1)}, bf16[8,48,3072]{2,1,0:T(8,128)(2,1)}, u32[]{:S(2)}) copy-start(bf16[8,48,3072]{2,1,0:T(8,128)(2,1)} %get-tuple-element.62) | copy-start | bytes 7077892
  208.7 29.0 %collective-permute-start.13 = (bf16[4,192,768]{2,1,0:T(8,128)(2,1)S(1)}, bf16[4,192,768]{2,1,0:T(8,128)(2,1)S(1)}, u32[]{:S(2)}, u32[]{:S(2)}) collective-permute-start(bf16[4,192,768]{2,1,0:T(8,128)(2,1)S(1)} %fusion.5), channel_id=1, source_target_pairs={{0,2},{1,3},{2,0},{3,1},{4,6},{5,7},{6,4},{7,5},{8,10},{9,11},{10,... | collective-permute-start | bytes 3538952 | tf_op jit(solution)/shard_map/ppermute | solution.py:769
  211.4 26.3 %copy-start.1 = (bf16[8,192,768]{2,1,0:T(8,128)(2,1)S(1)}, bf16[8,192,768]{2,1,0:T(8,128)(2,1)}, u32[]{:S(2)}) copy-start(bf16[8,192,768]{2,1,0:T(8,128)(2,1)} %get-tuple-element.64) | copy-start | bytes 7077892
  211.4 51.6 %collective-permute-start.3 = (bf16[4,48,3072]{2,1,0:T(8,128)(2,1)S(1)}, bf16[4,48,3072]{2,1,0:T(8,128)(2,1)S(1)}, u32[]{:S(2)}, u32[]{:S(2)}) collective-permute-start(bf16[4,48,3072]{2,1,0:T(8,128)(2,1)S(1)} %fusion.3), channel_id=1, source_target_pairs={{0,2},{1,3},{2,0},{3,1},{4,6},{5,7},{6,4},{7,5},{8,10},{9,11},{10,... | collective-permute-start | bytes 3538952 | tf_op jit(solution)/shard_map/ppermute | solution.py:769
  214.1 72.6 %collective-permute-start.8 = (bf16[4,48,3072]{2,1,0:T(8,128)(2,1)S(1)}, bf16[4,48,3072]{2,1,0:T(8,128)(2,1)S(1)}, u32[]{:S(2)}, u32[]{:S(2)}) collective-permute-start(bf16[4,48,3072]{2,1,0:T(8,128)(2,1)S(1)} %fusion.4), channel_id=1, source_target_pairs={{0,2},{1,3},{2,0},{3,1},{4,6},{5,7},{6,4},{7,5},{8,10},{9,11},{10,... | collective-permute-start | bytes 3538952 | tf_op jit(solution)/shard_map/ppermute | solution.py:769
  239.5 70.6 %collective-permute-start.14 = (bf16[192,768]{1,0:T(8,128)(2,1)S(1)}, bf16[192,768]{1,0:T(8,128)(2,1)S(1)}, u32[]{:S(2)}, u32[]{:S(2)}) collective-permute-start(bf16[192,768]{1,0:T(8,128)(2,1)S(1)} %get-tuple-element.69), channel_id=1, source_target_pairs={{0,4},{1,5},{2,6},{3,7},{4,0},{5,1},{6,2},{7,3},{8,12},{9,13},{10,... | collective-permute-start | bytes 884744 | tf_op jit(solution)/shard_map/ppermute | solution.py:769
  242.8 68.0 %collective-permute-start.16 = (bf16[192,768]{1,0:T(8,128)(2,1)S(1)}, bf16[192,768]{1,0:T(8,128)(2,1)S(1)}, u32[]{:S(2)}, u32[]{:S(2)}) collective-permute-start(bf16[192,768]{1,0:T(8,128)(2,1)S(1)} %get-tuple-element.70), channel_id=1, source_target_pairs={{0,12},{1,13},{2,14},{3,15},{4,8},{5,9},{6,10},{7,11},{8,4},{9,5},... | collective-permute-start | bytes 884744 | tf_op jit(solution)/shard_map/ppermute | solution.py:769
  264.9 24.4 %collective-permute-start.4 = (bf16[48,3072]{1,0:T(8,128)(2,1)S(1)}, bf16[48,3072]{1,0:T(8,128)(2,1)S(1)}, u32[]{:S(2)}, u32[]{:S(2)}) collective-permute-start(bf16[48,3072]{1,0:T(8,128)(2,1)S(1)} %get-tuple-element.75), channel_id=1, source_target_pairs={{0,4},{1,5},{2,6},{3,7},{4,0},{5,1},{6,2},{7,3},{8,12},{9,13},{10,... | collective-permute-start | bytes 884744 | tf_op jit(solution)/shard_map/ppermute | solution.py:769
  268.2 22.2 %collective-permute-start.6 = (bf16[48,3072]{1,0:T(8,128)(2,1)S(1)}, bf16[48,3072]{1,0:T(8,128)(2,1)S(1)}, u32[]{:S(2)}, u32[]{:S(2)}) collective-permute-start(bf16[48,3072]{1,0:T(8,128)(2,1)S(1)} %get-tuple-element.76), channel_id=1, source_target_pairs={{0,12},{1,13},{2,14},{3,15},{4,8},{5,9},{6,10},{7,11},{8,4},{9,5},... | collective-permute-start | bytes 884744 | tf_op jit(solution)/shard_map/ppermute | solution.py:769
  286.7 20.8 %collective-permute-start.5 = (bf16[48,3072]{1,0:T(8,128)(2,1)S(1)}, bf16[48,3072]{1,0:T(8,128)(2,1)S(1)}, u32[]{:S(2)}, u32[]{:S(2)}) collective-permute-start(bf16[48,3072]{1,0:T(8,128)(2,1)S(1)} %get-tuple-element.77), channel_id=1, source_target_pairs={{0,8},{1,9},{2,10},{3,11},{4,12},{5,13},{6,14},{7,15},{8,0},{9,1},... | collective-permute-start | bytes 884744 | tf_op jit(solution)/shard_map/ppermute | solution.py:769
  289.2 37.2 %collective-permute-start.15 = (bf16[192,768]{1,0:T(8,128)(2,1)S(1)}, bf16[192,768]{1,0:T(8,128)(2,1)S(1)}, u32[]{:S(2)}, u32[]{:S(2)}) collective-permute-start(bf16[192,768]{1,0:T(8,128)(2,1)S(1)} %get-tuple-element.71), channel_id=1, source_target_pairs={{0,8},{1,9},{2,10},{3,11},{4,12},{5,13},{6,14},{7,15},{8,0},{9,1},... | collective-permute-start | bytes 884744 | tf_op jit(solution)/shard_map/ppermute | solution.py:769
  290.4 37.0 %collective-permute-start.9 = (bf16[48,3072]{1,0:T(8,128)(2,1)S(1)}, bf16[48,3072]{1,0:T(8,128)(2,1)S(1)}, u32[]{:S(2)}, u32[]{:S(2)}) collective-permute-start(bf16[48,3072]{1,0:T(8,128)(2,1)S(1)} %get-tuple-element.72), channel_id=1, source_target_pairs={{0,4},{1,5},{2,6},{3,7},{4,0},{5,1},{6,2},{7,3},{8,12},{9,13},{10,... | collective-permute-start | bytes 884744 | tf_op jit(solution)/shard_map/ppermute | solution.py:769
  307.5 19.9 %collective-permute-start.11 = (bf16[48,3072]{1,0:T(8,128)(2,1)S(1)}, bf16[48,3072]{1,0:T(8,128)(2,1)S(1)}, u32[]{:S(2)}, u32[]{:S(2)}) collective-permute-start(bf16[48,3072]{1,0:T(8,128)(2,1)S(1)} %get-tuple-element.73), channel_id=1, source_target_pairs={{0,12},{1,13},{2,14},{3,15},{4,8},{5,9},{6,10},{7,11},{8,4},{9,5},... | collective-permute-start | bytes 884744 | tf_op jit(solution)/shard_map/ppermute | solution.py:769
  310.1 28.9 %collective-permute-start.10 = (bf16[48,3072]{1,0:T(8,128)(2,1)S(1)}, bf16[48,3072]{1,0:T(8,128)(2,1)S(1)}, u32[]{:S(2)}, u32[]{:S(2)}) collective-permute-start(bf16[48,3072]{1,0:T(8,128)(2,1)S(1)} %get-tuple-element.74), channel_id=1, source_target_pairs={{0,8},{1,9},{2,10},{3,11},{4,12},{5,13},{6,14},{7,15},{8,0},{9,1},... | collective-permute-start | bytes 884744 | tf_op jit(solution)/shard_map/ppermute | solution.py:769
Sparse Core Ops, SparseCore 0:
  117.8 85.6 all-reduce.4
